TPU v7x, 512 devices: a whole 4x8x8 slice. The times are simulated.
512 devices in a mesh: party: 2 (over z_lo), sample: 32 (over x, z_hi, core), feat: 8 (over y).
Axes of the slice: x: 4, y: 8, z: 8 (z_hi: 4, z_lo: 2; z = z_hi * 2 + z_lo), core: 2. Of those that a mesh axis runs over, the one named last changes fastest.
Arguments:
- x_share: bfloat16 [2, 8192, 8192], P('party', 'sample', 'feat'), may hold values from -3 to 3
- a_share: bfloat16 [2, 8192, 8192], P('party', 'sample', 'feat'), may hold values from -3 to 3
- w_share: float32 [2, 8192, 256], P('party', 'feat'), may hold values from -0.0625 to 0.0625
- b_share: bfloat16 [2, 8192, 256], P('party', 'feat'), may hold values from -0.0625 to 0.0625
- c_share: bfloat16 [2, 8192, 256], P('party', 'sample'), may hold values from -6 to 6
- mask_lin: bfloat16 [2, 8192, 256], P('party', 'sample'), may hold values from -12 to 12
- mask_sq: bfloat16 [2, 8192, 256], P('party', 'sample'), may hold values from -30 to 30
- mask_cube: bfloat16 [2, 8192, 256], P('party', 'sample'), may hold values from -240 to 240
- y_share: bfloat16 [2, 8192, 256], P('party', 'sample'), may hold values from -6 to 6
- r_mask: bfloat16 [2, 8192, 256], P('party', 'sample'), may hold values from -3 to 3
- grad_product: bfloat16 [2, 8192, 256], P('party', 'feat'), may hold values from -240 to 240
Outputs:
- new_weights: float32 [2, 8192, 256], P('party', 'feat')
All inputs are finite; a program needn't handle non-finite values.
Results may differ from a plain program's by a relative error of at most 0.0018.
Values may be sent and summed in bfloat16 or wider, within the bound.
A program may use at most 64 MiB of HBM per device.

v0:
```python
import jax
import jax.numpy as jnp
from jax import lax
from jax.sharding import Mesh
from jax.sharding import PartitionSpec as P

SAMPLE = ("sample_0", "sample_1", "sample_2")


learn_rate = 64.0
slope_one = 0.197
cube_coef = 0.004


def from_partner(shard, axis, bit):
    return lax.ppermute(shard, axis, [(i, i ^ 1 << bit) for i in range(lax.axis_size(axis))])


def sent_to_all(shard, axis):
    copies = jnp.broadcast_to(shard, (lax.axis_size(axis), *shard.shape))
    return lax.all_to_all(copies, axis, split_axis=0, concat_axis=0, tiled=True)


def laid_out(parts, dim):
    dims = list(parts.shape[1:])
    dims[dim] *= parts.shape[0]
    return jnp.moveaxis(parts, 0, dim).reshape(dims)


def collect(shard, axis, dim):
    parts = sent_to_all(shard, axis)
    return laid_out(parts, dim)


def over_copies(shard, axis):
    everything = sent_to_all(shard, axis)
    return jnp.sum(everything, axis=0)


def filled_up(lines, count):
    spare = -lines.shape[0] % count
    if not spare:
        return lines
    return jnp.concatenate([lines, jnp.zeros((spare, *lines.shape[1:]), lines.dtype)])


def gathered_by_axis(shard, axes, dim):
    far, near = axes
    first = sent_to_all(shard, far)
    parts = jnp.swapaxes(sent_to_all(first, near), 0, 1)
    return laid_out(parts.reshape(-1, *shard.shape), dim)


def in_blocks(shard, dim, count):
    before, after = (shard.shape[:dim], shard.shape[dim + 1 :])
    return jnp.moveaxis(shard.reshape(*before, count, -1, *after), dim, 0)


def sent_and_summed(shard, axis, dim):
    count = lax.axis_size(axis)
    parts = lax.all_to_all(in_blocks(shard, dim, count), axis, 0, 0, tiled=True)
    return jnp.sum(parts, axis=0)


def sum_by_axis(shard, axes, dim):
    far, near = axes
    parts = in_blocks(shard, dim, lax.axis_size(far))
    nearer = sent_and_summed(parts, near, dim + 1)
    arrived = lax.all_to_all(nearer, far, split_axis=0, concat_axis=0, tiled=True)
    return arrived.sum(axis=0)


def total_of(shard, axes):
    lines = shard.reshape(-1, shard.shape[-1])
    padded = filled_up(lines, lax.axis_size(axes[0]) * lax.axis_size(axes[1]))
    whole = gathered_by_axis(sum_by_axis(padded, axes, 0), axes, 0)
    return lax.slice_in_dim(whole, 0, len(lines)).reshape(shard.shape)


def take_rows(array, first, number):
    return lax.dynamic_slice_in_dim(array, first, number, 0)


def contract_rows(left, right):
    return lax.dot_general(
        left, right, (((0,), (0,)), ((), ())), preferred_element_type=jnp.float32
    )


def residual_open(summed, c_part, lin_part, sq_part, cube_part, label_part, mask_part, select):
    margin = summed + c_part.astype(jnp.float32)
    linear = lin_part.astype(jnp.float32)
    masked_margin = margin - linear
    other_margin = from_partner(masked_margin, "party", 0)
    spread = masked_margin + other_margin
    cubed = select * (spread * spread * spread) + 3.0 * (spread * spread) * linear
    cubed = cubed + 3.0 * spread * sq_part.astype(jnp.float32) + cube_part.astype(jnp.float32)
    residual = (
        0.5 * select + slope_one * margin - cube_coef * cubed - label_part.astype(jnp.float32)
    )
    masked_residual = (residual - mask_part.astype(jnp.float32)).astype(jnp.bfloat16)
    other_residual = from_partner(masked_residual, "party", 0)
    return (masked_residual.astype(jnp.float32) + other_residual.astype(jnp.float32)).astype(
        jnp.bfloat16
    )


def shards(
    x_share,
    a_share,
    w_share,
    b_share,
    c_share,
    mask_lin,
    mask_sq,
    mask_cube,
    y_share,
    r_mask,
    grad_product,
):
    select = (lax.axis_index("party") == 0).astype(jnp.float32)
    own_inputs = a_share[0]
    masked_inputs = (x_share[0].astype(jnp.float32) - own_inputs.astype(jnp.float32)).astype(
        jnp.bfloat16
    )
    block_width = w_share.shape[1]
    slab_rows = block_width // lax.axis_size(SAMPLE)
    sample_index = lax.axis_index(SAMPLE)
    slab_first = sample_index * slab_rows
    w_slab = take_rows(w_share[0], slab_first, slab_rows)
    b_slab = take_rows(b_share[0], slab_first, slab_rows)
    masked_slab = (w_slab - b_slab.astype(jnp.float32)).astype(jnp.bfloat16)
    other_inputs, other_slab = from_partner((masked_inputs, masked_slab), "party", 0)
    opened_inputs = (masked_inputs.astype(jnp.float32) + other_inputs.astype(jnp.float32)).astype(
        jnp.bfloat16
    )
    opened_slab = (masked_slab.astype(jnp.float32) + other_slab.astype(jnp.float32)).astype(
        jnp.bfloat16
    )
    starting = jnp.dot(opened_inputs, b_share[0], preferred_element_type=jnp.float32)
    running = starting
    piece = collect(opened_slab, SAMPLE, 0)
    opened_cols = opened_inputs
    share_cols = own_inputs
    running = running + select * jnp.dot(opened_cols, piece, preferred_element_type=jnp.float32)
    margin_part = running + jnp.dot(share_cols, piece, preferred_element_type=jnp.float32)
    margin_whole = over_copies(margin_part, "feat")
    opened_residual = residual_open(
        margin_whole,
        c_share[0],
        mask_lin[0],
        mask_sq[0],
        mask_cube[0],
        y_share[0],
        r_mask[0],
        select,
    )
    own_mask = r_mask[0]
    samples = opened_inputs.shape[0] * lax.axis_size(SAMPLE)
    opened_cols = opened_inputs
    share_cols = own_inputs
    term = select * contract_rows(opened_cols, opened_residual)
    term = term + contract_rows(opened_cols, own_mask)
    whole_grad = total_of(
        term + contract_rows(share_cols, opened_residual), (("sample_0", "sample_1"), "sample_2")
    )
    whole_grad = whole_grad + grad_product[0].astype(jnp.float32)
    updated = w_share[0] - learn_rate / samples * whole_grad
    return updated[None]


def solution(mesh):
    torus = Mesh(
        mesh.devices.reshape(mesh.shape["party"], 4, 4, 2, mesh.shape["feat"]),
        ("party", "sample_0", "sample_1", "sample_2", "feat"),
    )
    return jax.shard_map(
        shards,
        mesh=torus,
        in_specs=(
            P("party", SAMPLE, "feat"),
            P("party", SAMPLE, "feat"),
            P("party", "feat", None),
            P("party", "feat", None),
            P("party", SAMPLE, None),
            P("party", SAMPLE, None),
            P("party", SAMPLE, None),
            P("party", SAMPLE, None),
            P("party", SAMPLE, None),
            P("party", SAMPLE, None),
            P("party", "feat", None),
        ),
        out_specs=P("party", "feat", None),
        check_vma=False,
    )
```

profile of v0, /device:TPU:1, one launch (start us, length us, event | category | flops | bytes accessed | tf_op | source)
XLA Modules:
  0.0 182.8 jit_solution(1946659922156176859)
XLA Ops:
  0.0 0.0 copy-start.3
  0.0 0.0 copy-start
  0.0 0.9 fusion.18
  0.9 4.8 %collective-permute-start.1 = (bf16[32,256]{1,0:T(8,128)(2,1)S(1)}, bf16[32,256]{1,0:T(8,128)(2,1)S(1)}, u32[]{:S(2)}, u32[]{:S(2)}) collective-permute-start(bf16[32,256]{1,0:T(8,128)(2,1)S(1)} %fusion.18), channel_id=1, source_target_pairs={{0,256},{256,0},{1,257},{257,1},{2,258},{258,2},{3,259},{259,3},{4... | collective-permute-start | bytes 49160 | tf_op jit(solution)/shard_map/ppermute | solution.py:16
  5.7 1.1 collective-permute-done.1
  6.8 0.9 broadcast_in_dim.13
  7.7 14.1 %all-to-all-start = ((bf16[32,32,256]{2,1,0:T(8,128)(2,1)}), bf16[32,32,256]{2,1,0:T(8,128)(2,1)S(1)}, u32[]{:S(2)}, u32[]{:S(2)}) async-start(bf16[32,32,256]{2,1,0:T(8,128)(2,1)} %broadcast_in_dim.13), calls=%async_computation | async-start | bytes 1048576 | tf_op jit(solution)/shard_map/all_to_all | solution.py:21
  21.8 0.0 copy-done.3
  21.8 0.0 copy-done
  21.8 0.2 fusion.3
  22.0 3.1 %collective-permute-start = (bf16[256,1024]{1,0:T(8,128)(2,1)S(1)}, bf16[256,1024]{1,0:T(8,128)(2,1)S(1)}, u32[]{:S(2)}, u32[]{:S(2)}) collective-permute-start(bf16[256,1024]{1,0:T(8,128)(2,1)S(1)} %fusion.3), channel_id=1, source_target_pairs={{0,256},{256,0},{1,257},{257,1},{2,258},{258,2},{3,259},{259,3},{4... | collective-permute-start | bytes 1572872 | tf_op jit(solution)/shard_map/ppermute | solution.py:16
  25.1 0.0 copy-start.2
  25.1 21.4 %collective-permute-done = bf16[256,1024]{1,0:T(8,128)(2,1)S(1)} collective-permute-done((bf16[256,1024]{1,0:T(8,128)(2,1)S(1)}, bf16[256,1024]{1,0:T(8,128)(2,1)S(1)}, u32[]{:S(2)}, u32[]{:S(2)}) %collective-permute-start) | collective-permute-done | bytes 524320 | tf_op jit(solution)/shard_map/ppermute | solution.py:16
  46.5 0.2 add_convert_fusion
  46.7 0.0 all-to-all-done
  46.7 0.3 convolution_bitcast_fusion.1
  47.1 0.3 convolution_multiply_fusion.1
  47.4 0.0 copy-done.2
  47.4 0.3 fusion.2
  47.7 0.2 broadcast_in_dim.14
  47.9 56.3 %all_to_all.30 = f32[8,256,256]{2,1,0:T(8,128)S(1)} all-to-all(f32[8,256,256]{2,1,0:T(8,128)S(1)} %broadcast_in_dim.14), channel_id=1, replica_groups=mesh['party'=2,'sample_0'=4,'sample_1'=4,'sample_2'=2,'feat'=8] {'feat'}, dimensions={0} | all-to-all | bytes 4194304 | tf_op jit(solution)/shard_map/all_to_all | solution.py:21
  104.2 0.0 copy-start.5
  104.2 0.1 reduce_sum.27
  104.3 0.8 copy-done.5
  105.1 0.0 copy-start.6
  105.1 1.0 convert_subtract_fusion.1
  106.0 2.2 %collective-permute-start.2 = (f32[256,256]{1,0:T(8,128)S(1)}, f32[256,256]{1,0:T(8,128)S(1)}, u32[]{:S(2)}, u32[]{:S(2)}) collective-permute-start(f32[256,256]{1,0:T(8,128)S(1)} %convert_subtract_fusion.1), channel_id=1, source_target_pairs={{0,256},{256,0},{1,257},{257,1},{2,258},{258,2},{3,259},{259,3},{4... | collective-permute-start | bytes 786440 | tf_op jit(solution)/shard_map/ppermute | solution.py:16
  108.2 4.9 %collective-permute-done.2 = f32[256,256]{1,0:T(8,128)S(1)} collective-permute-done((f32[256,256]{1,0:T(8,128)S(1)}, f32[256,256]{1,0:T(8,128)S(1)}, u32[]{:S(2)}, u32[]{:S(2)}) %collective-permute-start.2) | collective-permute-done | bytes 262176 | tf_op jit(solution)/shard_map/ppermute | solution.py:16
  113.2 1.4 fusion.14
  114.5 2.2 %collective-permute-start.3 = (bf16[256,256]{1,0:T(8,128)(2,1)S(1)}, bf16[256,256]{1,0:T(8,128)(2,1)S(1)}, u32[]{:S(2)}, u32[]{:S(2)}) collective-permute-start(bf16[256,256]{1,0:T(8,128)(2,1)S(1)} %fusion.14), channel_id=1, source_target_pairs={{0,256},{256,0},{1,257},{257,1},{2,258},{258,2},{3,259},{259,3},{4... | collective-permute-start | bytes 393224 | tf_op jit(solution)/shard_map/ppermute | solution.py:16
  116.7 0.0 copy-done.6
  116.7 0.4 fusion.16
  117.1 3.2 %collective-permute-done.3 = bf16[256,256]{1,0:T(8,128)(2,1)S(1)} collective-permute-done((bf16[256,256]{1,0:T(8,128)(2,1)S(1)}, bf16[256,256]{1,0:T(8,128)(2,1)S(1)}, u32[]{:S(2)}, u32[]{:S(2)}) %collective-permute-start.3) | collective-permute-done | bytes 131104 | tf_op jit(solution)/shard_map/ppermute | solution.py:16
  120.3 0.3 convolution_bitcast_fusion
  120.6 0.4 fusion.1
  121.0 0.1 copy.28
  121.1 9.0 %all_to_all.31 = f32[2,16,32,256]{3,2,1,0:T(8,128)S(1)} all-to-all(f32[2,16,32,256]{3,2,1,0:T(8,128)S(1)} %bitcast.60), channel_id=1, replica_groups=mesh['party'=2,'sample_0'=4,'sample_1'=4,'sample_2'=2,'feat'=8] {'sample..., dimensions={0} | all-to-all | bytes 2097152 | tf_op jit(solution)/shard_map/all_to_all | solution.py:61
  130.1 0.1 reduce_sum.28
  130.2 23.5 %all_to_all.32 = f32[16,32,256]{2,1,0:T(8,128)S(1)} all-to-all(f32[16,32,256]{2,1,0:T(8,128)S(1)} %reduce_sum.28), channel_id=1, replica_groups=mesh['party'=2,'sample_0'=4,'sample_1'=4,'sample_2'=2,'feat'=8] {'sample..., dimensions={0} | all-to-all | bytes 1048576 | tf_op jit(solution)/shard_map/all_to_all | solution.py:69
  153.8 21.4 %all_to_all.33 = f32[16,32,256]{2,1,0:T(8,128)S(1)} all-to-all(f32[16,32,256]{2,1,0:T(8,128)S(1)} %broadcast_in_dim.15), channel_id=1, replica_groups=mesh['party'=2,'sample_0'=4,'sample_1'=4,'sample_2'=2,'feat'=8] {'sample..., dimensions={0} | all-to-all | bytes 1048576 | tf_op jit(solution)/shard_map/all_to_all | solution.py:21
  175.2 0.1 broadcast_in_dim.16
  175.4 0.0 copy-start.1
  175.4 0.0 copy-start.4
  175.4 6.1 %all_to_all.34 = f32[2,16,32,256]{3,2,1,0:T(8,128)S(1)} all-to-all(f32[2,16,32,256]{3,2,1,0:T(8,128)S(1)} %broadcast_in_dim.16), channel_id=1, replica_groups=mesh['party'=2,'sample_0'=4,'sample_1'=4,'sample_2'=2,'feat'=8] {'sample..., dimensions={0} | all-to-all | bytes 2097152 | tf_op jit(solution)/shard_map/all_to_all | solution.py:21
  181.5 0.1 copy.24
  181.6 0.0 copy-done.1
  181.6 0.0 copy-done.4
  181.6 1.2 multiply_subtract_fusion
  (3 shorter events, 0.1 us)
Async XLA Ops:
  0.0 21.8 %copy-start.3 = (bf16[1,256,1024]{2,1,0:T(8,128)(2,1)S(1)}, bf16[1,256,1024]{2,1,0:T(8,128)(2,1)}, u32[]{:S(2)}) copy-start(bf16[1,256,1024]{2,1,0:T(8,128)(2,1)} %param.11) | copy-start | bytes 1572868
  0.0 21.8 %copy-start = (bf16[1,256,1024]{2,1,0:T(8,128)(2,1)S(1)}, bf16[1,256,1024]{2,1,0:T(8,128)(2,1)}, u32[]{:S(2)}) copy-start(bf16[1,256,1024]{2,1,0:T(8,128)(2,1)} %param.12) | copy-start | bytes 1572868
  0.9 5.9 %collective-permute-start.1 = (bf16[32,256]{1,0:T(8,128)(2,1)S(1)}, bf16[32,256]{1,0:T(8,128)(2,1)S(1)}, u32[]{:S(2)}, u32[]{:S(2)}) collective-permute-start(bf16[32,256]{1,0:T(8,128)(2,1)S(1)} %fusion.18), channel_id=1, source_target_pairs={{0,256},{256,0},{1,257},{257,1},{2,258},{258,2},{3,259},{259,3},{4... | collective-permute-start | bytes 49160 | tf_op jit(solution)/shard_map/ppermute | solution.py:16
  7.7 39.1 %all-to-all-start = ((bf16[32,32,256]{2,1,0:T(8,128)(2,1)}), bf16[32,32,256]{2,1,0:T(8,128)(2,1)S(1)}, u32[]{:S(2)}, u32[]{:S(2)}) async-start(bf16[32,32,256]{2,1,0:T(8,128)(2,1)} %broadcast_in_dim.13), calls=%async_computation | async-start | bytes 1048576 | tf_op jit(solution)/shard_map/all_to_all | solution.py:21
  22.0 24.5 %collective-permute-start = (bf16[256,1024]{1,0:T(8,128)(2,1)S(1)}, bf16[256,1024]{1,0:T(8,128)(2,1)S(1)}, u32[]{:S(2)}, u32[]{:S(2)}) collective-permute-start(bf16[256,1024]{1,0:T(8,128)(2,1)S(1)} %fusion.3), channel_id=1, source_target_pairs={{0,256},{256,0},{1,257},{257,1},{2,258},{258,2},{3,259},{259,3},{4... | collective-permute-start | bytes 1572872 | tf_op jit(solution)/shard_map/ppermute | solution.py:16
  25.1 22.2 %copy-start.2 = (bf16[1,1024,256]{2,1,0:T(8,128)(2,1)S(1)}, bf16[1,1024,256]{2,1,0:T(8,128)(2,1)}, u32[]{:S(2)}) copy-start(bf16[1,1024,256]{2,1,0:T(8,128)(2,1)} %param.14) | copy-start | bytes 1572868
  104.2 0.9 copy-start.5
  105.1 11.7 %copy-start.6 = (bf16[1,256,256]{2,1,0:T(8,128)(2,1)S(1)}, bf16[1,256,256]{2,1,0:T(8,128)(2,1)}, u32[]{:S(2)}) copy-start(bf16[1,256,256]{2,1,0:T(8,128)(2,1)} %param.20) | copy-start | bytes 393220
  106.0 7.1 %collective-permute-start.2 = (f32[256,256]{1,0:T(8,128)S(1)}, f32[256,256]{1,0:T(8,128)S(1)}, u32[]{:S(2)}, u32[]{:S(2)}) collective-permute-start(f32[256,256]{1,0:T(8,128)S(1)} %convert_subtract_fusion.1), channel_id=1, source_target_pairs={{0,256},{256,0},{1,257},{257,1},{2,258},{258,2},{3,259},{259,3},{4... | collective-permute-start | bytes 786440 | tf_op jit(solution)/shard_map/ppermute | solution.py:16
  114.5 5.7 %collective-permute-start.3 = (bf16[256,256]{1,0:T(8,128)(2,1)S(1)}, bf16[256,256]{1,0:T(8,128)(2,1)S(1)}, u32[]{:S(2)}, u32[]{:S(2)}) collective-permute-start(bf16[256,256]{1,0:T(8,128)(2,1)S(1)} %fusion.14), channel_id=1, source_target_pairs={{0,256},{256,0},{1,257},{257,1},{2,258},{258,2},{3,259},{259,3},{4... | collective-permute-start | bytes 393224 | tf_op jit(solution)/shard_map/ppermute | solution.py:16
  175.4 6.2 %copy-start.1 = (f32[1,1024,256]{2,1,0:T(8,128)S(1)}, f32[1,1024,256]{2,1,0:T(8,128)}, u32[]{:S(2)}) copy-start(f32[1,1024,256]{2,1,0:T(8,128)} %param.13) | copy-start | bytes 3145732
  175.4 6.2 %copy-start.4 = (bf16[1,1024,256]{2,1,0:T(8,128)(2,1)S(1)}, bf16[1,1024,256]{2,1,0:T(8,128)(2,1)}, u32[]{:S(2)}) copy-start(bf16[1,1024,256]{2,1,0:T(8,128)(2,1)} %param.21) | copy-start | bytes 1572868
where the time goes:
time: 184 us; the launch traced here: 183 us
  blocking collectives  116 us (63%)
  waiting for transfers between devices  30.6 us (17%)
  starting transfers between devices  26.4 us (14%)
  other arithmetic  5.06 us (3%)
  local copies, waits for them, and re-layouts  2.14 us (1%)
  matrix products  1.95 us (1%)
    all_to_all x3, blocking collectives, sent_to_all(): return lax.all_to_all(copies, axis, split_axis=0, concat_axis=0, tiled=True)  83.8 us
    ppermute x4, waiting for transfers between devices, from_partner(): lax.ppermute(shard, axis, [(i, i ^ 1 << bit) for i in range(lax.axis_size...  30.6 us
    all_to_all x1, blocking collectives, sum_by_axis(): lax.all_to_all(nearer, far, split_axis=0, concat_axis=0, tiled=True)  23.5 us
    all_to_all x1, starting transfers between devices, sent_to_all(): return lax.all_to_all(copies, axis, split_axis=0, concat_axis=0, tiled=True)  14.1 us
    ppermute x4, starting transfers between devices, from_partner(): lax.ppermute(shard, axis, [(i, i ^ 1 << bit) for i in range(lax.axis_size...  12.3 us
    all_to_all x1, blocking collectives, sent_and_summed(): parts = lax.all_to_all(in_blocks(shard, dim, count), axis, 0, 0, tiled=True)  9 us
  transfers between devices with their start and end apart: 5, of which 4 were waited for; matrix products, arithmetic and copies ran while one was open for 0% of the time, Pallas kernels for 0%

commit v1 on v0

v1 whole, which is shorter than its diff:
```python
import jax
import jax.numpy as jnp
from jax import lax
from jax.experimental import pallas as pl
from jax.experimental.pallas import tpu as pltpu
from jax.sharding import Mesh
from jax.sharding import PartitionSpec as P

SAMPLE = ("sample_0", "sample_1", "sample_2")
MESH = pl.DeviceIdType.MESH
F32 = jnp.float32
BF16 = jnp.bfloat16

learn_rate = 64.0
slope_one = 0.197
cube_coef = 0.004

ROWS = 256
COLS = 1024
PH = 256
CHUNK = 64
CHUNKS = ROWS // CHUNK
GROUP = 16
PIECE = ROWS // GROUP
HALF = COLS // 2
QUARTER = HALF // 4
LAST = QUARTER // 4
SMALL = 6
ORDER = (8, 7, 9, 6, 10, 5, 11, 4, 12, 3, 13, 2, 14, 1, 15)


def kernel(
    x_ref, a_ref, w_ref, b_ref, c_ref, lin_ref, sq_ref, cube_ref, y_ref, r_ref,
    grad_ref,
    xv, av, wv, bv, sv, mv, om, ev, et, at, wm, ow, opened, zv, zbuf, pack, pbuf,
    rbuf, gv, gbuf, xbuf, hv, hbuf,
    load_sem, in_send, in_recv, wt_send, wt_recv, pk_send, pk_recv,
    z_send, z_recv, r_send, r_recv, g_send, g_recv, x_send, x_recv, h_send, h_recv,
    f_send, f_recv, k_send, k_recv,
):
    party = lax.axis_index("party")
    xi = lax.axis_index("sample_0")
    hi = lax.axis_index("sample_1")
    core = lax.axis_index("sample_2")
    feat = lax.axis_index("feat")
    me = feat * 2 + party
    select = (party == 0).astype(F32)

    def at_place(p=None, x=None, h=None, c=None, f=None):
        return (
            party if p is None else p,
            xi if x is None else x,
            hi if h is None else h,
            core if c is None else c,
            feat if f is None else f,
        )

    def in_group(d):
        t = lax.rem(me + d, GROUP)
        return at_place(p=lax.rem(t, 2), f=lax.div(t, 2))

    partner = at_place(p=1 - party)
    sibling = at_place(c=1 - core)
    other_z = at_place(p=1 - party, h=lax.rem(hi + 3 + 2 * party, 4))
    across = [(dx, dh) for dx in range(4) for dh in range(4) if dx or dh]

    def at_sample(dx, dh):
        return at_place(x=lax.rem(xi + dx, 4), h=lax.rem(hi + dh, 4))

    loads = [
        pltpu.make_async_copy(src.at[0], dst, load_sem.at[i])
        for i, (src, dst) in enumerate(
            [(x_ref, xv), (a_ref, av), (w_ref, wv), (b_ref, bv)]
            + [
                (ref, sv.at[i])
                for i, ref in enumerate((c_ref, lin_ref, sq_ref, cube_ref, y_ref, r_ref))
            ]
        )
    ]
    for load in loads:
        load.start()

    greeted = [sibling, partner, other_z]
    greeted += [in_group(d) for d in ORDER if d != 1 and d != 15]
    greeted += [at_place(p=1 - party, f=lax.rem(feat + 7 + 2 * party, 8))]
    greeted += [at_sample(dx, dh) for dx, dh in across]
    barrier = pltpu.get_barrier_semaphore()
    for place in greeted:
        pl.semaphore_signal(barrier, inc=1, device_id=place, device_id_type=MESH)

    loads[0].wait()
    loads[1].wait()
    mv[...] = (xv[...].astype(F32) - av[...].astype(F32)).astype(BF16)
    loads[2].wait()
    loads[3].wait()
    wm[...] = (wv[...] - bv[...].astype(F32)).astype(BF16)
    pl.semaphore_wait(barrier, len(greeted))

    def remote(src, dst, send, recv, place):
        return pltpu.make_async_remote_copy(
            src_ref=src, dst_ref=dst, send_sem=send, recv_sem=recv,
            device_id=place, device_id_type=MESH,
        )

    inputs = []
    for k in range(CHUNKS):
        rows = pl.ds(k * CHUNK, CHUNK)
        inputs.append(remote(mv.at[rows], om.at[rows], in_send.at[k], in_recv.at[k], partner))
    my_half = pl.ds(pl.multiple_of(core * HALF, HALF), HALF)
    weights = remote(wm.at[my_half], ow.at[my_half], wt_send.at[0], wt_recv.at[0], other_z)
    weights.start()
    for copy in inputs:
        copy.start()

    for load in loads[4:]:
        load.wait()
    mine = pl.ds(pl.multiple_of(me * PIECE, PIECE), PIECE)
    theirs = pl.ds(
        pl.multiple_of((feat * 2 + 1 - party) * PIECE, PIECE), PIECE
    )
    for i in range(SMALL):
        pack[i] = sv[i, theirs, :]
    packed = remote(pack, pbuf, pk_send.at[0], pk_recv.at[0], partner)
    packed.start()

    at[...] = av[...].T
    weights.wait_recv()
    passed = remote(ow.at[my_half], ow.at[my_half], wt_send.at[1], wt_recv.at[1], sibling)
    passed.start()
    passed.wait()
    opened[...] = (wm[...].astype(F32) + ow[...].astype(F32)).astype(BF16)
    zv[...] = jnp.dot(av[...], opened[...], preferred_element_type=F32)

    for k in range(CHUNKS):
        rows = pl.ds(k * CHUNK, CHUNK)
        inputs[k].wait_recv()
        part = (mv[rows, :].astype(F32) + om[rows, :].astype(F32)).astype(BF16)
        ev[rows, :] = part
        both = select * jnp.dot(part, opened[...], preferred_element_type=F32)
        zv[rows, :] += both + jnp.dot(part, bv[...], preferred_element_type=F32)

    sums = {}
    for d in ORDER:
        t = lax.rem(me + d, GROUP)
        rows = pl.ds(pl.multiple_of(t * PIECE, PIECE), PIECE)
        sums[d] = remote(zv.at[rows], zbuf.at[d], z_send.at[d], z_recv.at[d], in_group(d))
        sums[d].start()

    et[...] = ev[...].T
    gv[...] = jnp.dot(et[...], sv[SMALL - 1], preferred_element_type=F32)
    packed.wait()

    own = zv[mine, :]
    for d in range(2, GROUP, 2):
        sums[d].wait_recv()
        own = own + zbuf[d]
    sums[1].wait_recv()
    far = zbuf[1]
    for d in range(3, GROUP, 2):
        sums[d].wait_recv()
        far = far + zbuf[d]

    def values(i):
        return sv[i, mine, :].astype(F32), pbuf[i].astype(F32)

    own_c, far_c = values(0)
    own_lin, far_lin = values(1)
    own_margin, far_margin = own + own_c, far + far_c
    spread = (own_margin - own_lin) + (far_margin - far_lin)

    def residual(s, margin, i):
        linear = values(1)[i]
        cubed = s * (spread * spread * spread) + 3.0 * (spread * spread) * linear
        cubed = cubed + 3.0 * spread * values(2)[i] + values(3)[i]
        result = 0.5 * s + slope_one * margin - cube_coef * cubed - values(4)[i]
        return (result - values(5)[i]).astype(BF16).astype(F32)

    rbuf[mine, :] = (residual(select, own_margin, 0) + residual(1.0 - select, far_margin, 1)).astype(
        BF16
    )
    spreads = {}
    for d in ORDER:
        spreads[d] = remote(
            rbuf.at[mine], rbuf.at[mine], r_send.at[d], r_recv.at[d], in_group(d)
        )
        spreads[d].start()
    for d in ORDER:
        spreads[d].wait_recv()

    def add_terms(first):
        rows = pl.ds(pl.multiple_of(first, HALF), HALF)
        term = select * jnp.dot(et[rows, :], rbuf[...], preferred_element_type=F32)
        gv[rows, :] += term + jnp.dot(at[rows, :], rbuf[...], preferred_element_type=F32)

    add_terms((1 - core) * HALF)
    their_half = pl.ds(pl.multiple_of((1 - core) * HALF, HALF), HALF)
    crossing = remote(gv.at[their_half], gbuf, g_send.at[0], g_recv.at[0], sibling)
    crossing.start()
    add_terms(core * HALF)
    crossing.wait_recv()
    gbuf[...] += gv[my_half, :]

    quarters = {}
    for d in (2, 1, 3):
        t = lax.rem(xi + d, 4)
        rows = pl.ds(pl.multiple_of(t * QUARTER, QUARTER), QUARTER)
        quarters[d] = remote(
            gbuf.at[rows], xbuf.at[d], x_send.at[d], x_recv.at[d], at_sample(d, 0)
        )
        quarters[d].start()
    total = gbuf[pl.ds(pl.multiple_of(xi * QUARTER, QUARTER), QUARTER), :]
    for d in (1, 3, 2):
        quarters[d].wait_recv()
        total = total + xbuf[d]
    hv[...] = total

    lasts = {}
    for d in (2, 1, 3):
        t = lax.rem(hi + d, 4)
        rows = pl.ds(pl.multiple_of(t * LAST, LAST), LAST)
        lasts[d] = remote(hv.at[rows], hbuf.at[d], h_send.at[d], h_recv.at[d], at_sample(0, d))
        lasts[d].start()
    total = hv[pl.ds(pl.multiple_of(hi * LAST, LAST), LAST), :]
    for d in (1, 3, 2):
        lasts[d].wait_recv()
        total = total + hbuf[d]

    place = pl.ds(pl.multiple_of(core * HALF + xi * QUARTER + hi * LAST, LAST), LAST)
    grad_ref[place, :] = total.astype(BF16)
    finals = []
    for i, (dx, dh) in enumerate(across):
        finals.append(
            remote(
                grad_ref.at[place], grad_ref.at[place], f_send.at[i], f_recv.at[i], at_sample(dx, dh)
            )
        )
    for copy in finals[::-1]:
        copy.start()
    for copy in finals:
        copy.wait_recv()
    ending = remote(grad_ref.at[my_half], grad_ref.at[my_half], k_send.at[0], k_recv.at[0], sibling)
    ending.start()

    weights.wait_send()
    for copy in inputs + [sums[d] for d in ORDER] + [spreads[d] for d in ORDER]:
        copy.wait_send()
    crossing.wait_send()
    for copy in [quarters[d] for d in (1, 2, 3)] + [lasts[d] for d in (1, 2, 3)] + finals:
        copy.wait_send()
    ending.wait()


def gradient(x, a, w, b, c, lin, sq, cube, y, r):
    dma = pltpu.SemaphoreType.DMA
    return pl.pallas_call(
        kernel,
        out_shape=jax.ShapeDtypeStruct((COLS, PH), BF16),
        in_specs=[pl.BlockSpec(memory_space=pl.ANY)] * 10,
        out_specs=pl.BlockSpec(memory_space=pltpu.VMEM),
        scratch_shapes=[
            pltpu.VMEM((ROWS, COLS), BF16),
            pltpu.VMEM((ROWS, COLS), BF16),
            pltpu.VMEM((COLS, PH), F32),
            pltpu.VMEM((COLS, PH), BF16),
            pltpu.VMEM((SMALL, ROWS, PH), BF16),
            pltpu.VMEM((ROWS, COLS), BF16),
            pltpu.VMEM((ROWS, COLS), BF16),
            pltpu.VMEM((ROWS, COLS), BF16),
            pltpu.VMEM((COLS, ROWS), BF16),
            pltpu.VMEM((COLS, ROWS), BF16),
            pltpu.VMEM((COLS, PH), BF16),
            pltpu.VMEM((COLS, PH), BF16),
            pltpu.VMEM((COLS, PH), BF16),
            pltpu.VMEM((ROWS, PH), F32),
            pltpu.VMEM((GROUP, PIECE, PH), F32),
            pltpu.VMEM((SMALL, PIECE, PH), BF16),
            pltpu.VMEM((SMALL, PIECE, PH), BF16),
            pltpu.VMEM((ROWS, PH), BF16),
            pltpu.VMEM((COLS, PH), F32),
            pltpu.VMEM((HALF, PH), F32),
            pltpu.VMEM((4, QUARTER, PH), F32),
            pltpu.VMEM((QUARTER, PH), F32),
            pltpu.VMEM((4, LAST, PH), F32),
            dma((10,)),
            dma((CHUNKS,)), dma((CHUNKS,)),
            dma((2,)), dma((2,)),
            dma((1,)), dma((1,)),
            dma((GROUP,)), dma((GROUP,)),
            dma((GROUP,)), dma((GROUP,)),
            dma((1,)), dma((1,)),
            dma((4,)), dma((4,)),
            dma((4,)), dma((4,)),
            dma((15,)), dma((15,)),
            dma((1,)), dma((1,)),
        ],
        compiler_params=pltpu.CompilerParams(
            collective_id=0, has_side_effects=True, vmem_limit_bytes=40 * 2**20
        ),
        cost_estimate=pl.CostEstimate(
            flops=12 * ROWS * COLS * PH, bytes_accessed=5 * 2**20, transcendentals=0
        ),
    )(x, a, w, b, c, lin, sq, cube, y, r)


def shards(x, a, w, b, c, lin, sq, cube, y, r, grad_product):
    grad = gradient(x, a, w, b, c, lin, sq, cube, y, r)
    samples = x.shape[1] * lax.axis_size(SAMPLE)
    whole = grad.astype(F32) + grad_product[0].astype(F32)
    return (w[0] - learn_rate / samples * whole)[None]


def solution(mesh):
    torus = Mesh(
        mesh.devices.reshape(mesh.shape["party"], 4, 4, 2, mesh.shape["feat"]),
        ("party", "sample_0", "sample_1", "sample_2", "feat"),
    )
    return jax.shard_map(
        shards,
        mesh=torus,
        in_specs=(
            P("party", SAMPLE, "feat"),
            P("party", SAMPLE, "feat"),
            P("party", "feat", None),
            P("party", "feat", None),
            P("party", SAMPLE, None),
            P("party", SAMPLE, None),
            P("party", SAMPLE, None),
            P("party", SAMPLE, None),
            P("party", SAMPLE, None),
            P("party", SAMPLE, None),
            P("party", "feat", None),
        ),
        out_specs=P("party", "feat", None),
        check_vma=False,
    )
```

time: 184 us -> 81.7 us (0.44)
  blocking collectives: 116 us -> 0 us
  Pallas kernels: 0 us -> 70.4 us
  waiting for transfers between devices: 30.6 us -> 0 us
  starting transfers between devices: 26.4 us -> 0 us
  local copies, waits for them, and re-layouts: 2.14 us -> 9.77 us
  other arithmetic: 5.06 us -> 1.14 us
  matrix products: 1.95 us -> 0 us
    all_to_all x5 -> x0, blocking collectives: 116 us -> none  [the longest x3 83.8 us: sent_to_all(): return lax.all_to_all(copies, axis, split_axis=0, concat_axis=0, tiled=True)]
    pallas_call x0 -> x1, Pallas kernels: none -> 70.4 us  [gradient(): pl.pallas_call(kernel, out_shape=jax.ShapeDtypeStruct((COLS, PH), BF16),...]
    ppermute x4 -> x0, waiting for transfers between devices: 30.6 us -> none  [from_partner(): lax.ppermute(shard, axis, [(i, i ^ 1 << bit) for i in range(lax.axis_size...]
    all_to_all x1 -> x0, starting transfers between devices: 14.1 us -> none  [sent_to_all(): return lax.all_to_all(copies, axis, split_axis=0, concat_axis=0, tiled=True)]
    ppermute x4 -> x0, starting transfers between devices: 12.3 us -> none  [from_partner(): lax.ppermute(shard, axis, [(i, i ^ 1 << bit) for i in range(lax.axis_size...]
    unnamed x14 -> x22, local copies, waits for them, and re-layouts: 0.78 us -> 9.77 us
    convert_element_type x5 -> x0, other arithmetic: 2.63 us -> none  [the longest x1 1.39 us: residual_open(): (residual - mask_part.astype(jnp.float32)).astype(jnp.bfloat16)]
    sub x2 -> x0, other arithmetic: 2.15 us -> none  [the longest x1 1.17 us: shards(): updated = w_share[0] - learn_rate / samples * whole_grad]
  transfers between devices with their start and end apart: 5 -> 0, of which waited for: 4 -> 0; matrix products, arithmetic and copies ran while one was open for 0% -> 0% of each run, Pallas kernels for 0% -> 0%
where the time goes in v1:
time: 81.7 us; the launch traced here: 81.3 us
  Pallas kernels  70.4 us (86%)
  local copies, waits for them, and re-layouts  9.77 us (12%)
  other arithmetic  1.14 us (1%)
    pallas_call x1, Pallas kernels, gradient(): pl.pallas_call(kernel, out_shape=jax.ShapeDtypeStruct((COLS, PH), BF16),...  70.4 us
    unnamed x22, local copies, waits for them, and re-layouts  9.77 us

profile of v1, /device:TPU:1, one launch (start us, length us, event | category | flops | bytes accessed | tf_op | source)
XLA Modules:
  0.0 81.3 jit_solution(5247301772521332121)
XLA Ops:
  0.0 0.0 copy-start
  0.0 1.2 %copy-done = f32[1,1024,256]{2,1,0:T(8,128)S(1)} copy-done((f32[1,1024,256]{2,1,0:T(8,128)S(1)}, f32[1,1024,256]{2,1,0:T(8,128)}, u32[]{:S(2)}) %copy-start) | copy-done | bytes 1048600
  1.2 0.0 copy-start.1
  1.2 1.0 %copy-done.1 = bf16[1,256,1024]{2,1,0:T(8,128)(2,1)S(1)} copy-done((bf16[1,256,1024]{2,1,0:T(8,128)(2,1)S(1)}, bf16[1,256,1024]{2,1,0:T(8,128)(2,1)}, u32[]{:S(2)}) %copy-start.1) | copy-done | bytes 524312
  2.3 0.0 copy-start.2
  2.3 1.0 %copy-done.2 = bf16[1,256,1024]{2,1,0:T(8,128)(2,1)S(1)} copy-done((bf16[1,256,1024]{2,1,0:T(8,128)(2,1)S(1)}, bf16[1,256,1024]{2,1,0:T(8,128)(2,1)}, u32[]{:S(2)}) %copy-start.2) | copy-done | bytes 524312
  3.3 0.0 copy-start.3
  3.3 1.0 %copy-done.3 = bf16[1,1024,256]{2,1,0:T(8,128)(2,1)S(1)} copy-done((bf16[1,1024,256]{2,1,0:T(8,128)(2,1)S(1)}, bf16[1,1024,256]{2,1,0:T(8,128)(2,1)}, u32[]{:S(2)}) %copy-start.3) | copy-done | bytes 524312
  4.4 0.0 copy-start.4
  4.4 0.9 %copy-done.4 = bf16[1,256,256]{2,1,0:T(8,128)(2,1)S(1)} copy-done((bf16[1,256,256]{2,1,0:T(8,128)(2,1)S(1)}, bf16[1,256,256]{2,1,0:T(8,128)(2,1)}, u32[]{:S(2)}) %copy-start.4) | copy-done | bytes 131096
  5.3 0.0 copy-start.5
  5.3 0.9 %copy-done.5 = bf16[1,256,256]{2,1,0:T(8,128)(2,1)S(1)} copy-done((bf16[1,256,256]{2,1,0:T(8,128)(2,1)S(1)}, bf16[1,256,256]{2,1,0:T(8,128)(2,1)}, u32[]{:S(2)}) %copy-start.5) | copy-done | bytes 131096
  6.2 0.0 copy-start.6
  6.2 0.9 %copy-done.6 = bf16[1,256,256]{2,1,0:T(8,128)(2,1)S(1)} copy-done((bf16[1,256,256]{2,1,0:T(8,128)(2,1)S(1)}, bf16[1,256,256]{2,1,0:T(8,128)(2,1)}, u32[]{:S(2)}) %copy-start.6) | copy-done | bytes 131096
  7.1 0.0 copy-start.7
  7.1 0.9 %copy-done.7 = bf16[1,256,256]{2,1,0:T(8,128)(2,1)S(1)} copy-done((bf16[1,256,256]{2,1,0:T(8,128)(2,1)S(1)}, bf16[1,256,256]{2,1,0:T(8,128)(2,1)}, u32[]{:S(2)}) %copy-start.7) | copy-done | bytes 131096
  8.0 0.0 copy-start.8
  8.0 0.9 %copy-done.8 = bf16[1,256,256]{2,1,0:T(8,128)(2,1)S(1)} copy-done((bf16[1,256,256]{2,1,0:T(8,128)(2,1)S(1)}, bf16[1,256,256]{2,1,0:T(8,128)(2,1)}, u32[]{:S(2)}) %copy-start.8) | copy-done | bytes 131096
  8.9 0.0 copy-start.9
  8.9 0.9 %copy-done.9 = bf16[1,256,256]{2,1,0:T(8,128)(2,1)S(1)} copy-done((bf16[1,256,256]{2,1,0:T(8,128)(2,1)S(1)}, bf16[1,256,256]{2,1,0:T(8,128)(2,1)}, u32[]{:S(2)}) %copy-start.9) | copy-done | bytes 131096
  9.8 0.0 copy-start.10
  9.8 70.4 %shard_map.109 = bf16[1024,256]{1,0:T(8,128)(2,1)S(1)} custom-call(bf16[1,256,1024]{2,1,0:T(8,128)(2,1)S(1)} %copy-done.1, bf16[1,256,1024]{2,1,0:T(8,128)(2,1)S(1)} %copy-done.2, f32[1,1024,256]{2,1,0:T(8,128)S(1)} %copy-done, bf16[1,1024,256]{2,1,0:T(8,128)(2,1)S(1)} %copy-done.3, bf16[1,256,256]{2,1,0:T(8,128)(2,1)S(1)} %copy-done.4, ...), custom_call_target="tpu_custom_call" | custom-call | flops 805306368 | bytes 5242880 | tf_op jit(solution)/shard_map/pallas_call | solution.py:255
  80.2 0.0 copy-done.10
  80.2 1.1 %fusion.2 = f32[1,1024,256]{2,1,0:T(8,128)} fusion(f32[1,1024,256]{2,1,0:T(8,128)S(1)} %copy-done, bf16[1024,256]{1,0:T(8,128)(2,1)S(1)} %shard_map.109, bf16[1,1024,256]{2,1,0:T(8,128)(2,1)S(1)} %copy-done.10), kind=kLoop, calls=%fused_computation.3 | loop fusion | flops 1310720 | bytes 3145728 | tf_op jit(solution)/shard_map/broadcast_in_dim | solution.py:309
Async XLA Ops:
  0.0 1.2 %copy-start = (f32[1,1024,256]{2,1,0:T(8,128)S(1)}, f32[1,1024,256]{2,1,0:T(8,128)}, u32[]{:S(2)}) copy-start(f32[1,1024,256]{2,1,0:T(8,128)} %w_ref.1) | copy-start | bytes 3145732
  1.2 1.0 %copy-start.1 = (bf16[1,256,1024]{2,1,0:T(8,128)(2,1)S(1)}, bf16[1,256,1024]{2,1,0:T(8,128)(2,1)}, u32[]{:S(2)}) copy-start(bf16[1,256,1024]{2,1,0:T(8,128)(2,1)} %x_ref.1) | copy-start | bytes 1572868
  2.3 1.0 %copy-start.2 = (bf16[1,256,1024]{2,1,0:T(8,128)(2,1)S(1)}, bf16[1,256,1024]{2,1,0:T(8,128)(2,1)}, u32[]{:S(2)}) copy-start(bf16[1,256,1024]{2,1,0:T(8,128)(2,1)} %a_ref.1) | copy-start | bytes 1572868
  3.3 1.0 %copy-start.3 = (bf16[1,1024,256]{2,1,0:T(8,128)(2,1)S(1)}, bf16[1,1024,256]{2,1,0:T(8,128)(2,1)}, u32[]{:S(2)}) copy-start(bf16[1,1024,256]{2,1,0:T(8,128)(2,1)} %b_ref.1) | copy-start | bytes 1572868
  4.4 0.9 %copy-start.4 = (bf16[1,256,256]{2,1,0:T(8,128)(2,1)S(1)}, bf16[1,256,256]{2,1,0:T(8,128)(2,1)}, u32[]{:S(2)}) copy-start(bf16[1,256,256]{2,1,0:T(8,128)(2,1)} %c_ref.1) | copy-start | bytes 393220
  5.3 0.9 %copy-start.5 = (bf16[1,256,256]{2,1,0:T(8,128)(2,1)S(1)}, bf16[1,256,256]{2,1,0:T(8,128)(2,1)}, u32[]{:S(2)}) copy-start(bf16[1,256,256]{2,1,0:T(8,128)(2,1)} %lin_ref.1) | copy-start | bytes 393220
  6.2 0.9 %copy-start.6 = (bf16[1,256,256]{2,1,0:T(8,128)(2,1)S(1)}, bf16[1,256,256]{2,1,0:T(8,128)(2,1)}, u32[]{:S(2)}) copy-start(bf16[1,256,256]{2,1,0:T(8,128)(2,1)} %sq_ref.1) | copy-start | bytes 393220
  7.1 0.9 %copy-start.7 = (bf16[1,256,256]{2,1,0:T(8,128)(2,1)S(1)}, bf16[1,256,256]{2,1,0:T(8,128)(2,1)}, u32[]{:S(2)}) copy-start(bf16[1,256,256]{2,1,0:T(8,128)(2,1)} %cube_ref.1) | copy-start | bytes 393220
  8.0 0.9 %copy-start.8 = (bf16[1,256,256]{2,1,0:T(8,128)(2,1)S(1)}, bf16[1,256,256]{2,1,0:T(8,128)(2,1)}, u32[]{:S(2)}) copy-start(bf16[1,256,256]{2,1,0:T(8,128)(2,1)} %y_ref.1) | copy-start | bytes 393220
  8.9 0.9 %copy-start.9 = (bf16[1,256,256]{2,1,0:T(8,128)(2,1)S(1)}, bf16[1,256,256]{2,1,0:T(8,128)(2,1)}, u32[]{:S(2)}) copy-start(bf16[1,256,256]{2,1,0:T(8,128)(2,1)} %r_ref.1) | copy-start | bytes 393220
  9.8 70.4 %copy-start.10 = (bf16[1,1024,256]{2,1,0:T(8,128)(2,1)S(1)}, bf16[1,1024,256]{2,1,0:T(8,128)(2,1)}, u32[]{:S(2)}) copy-start(bf16[1,1024,256]{2,1,0:T(8,128)(2,1)} %param.21) | copy-start | bytes 1572868

commit v2 on v1

v2 whole, which is shorter than its diff:
```python
import jax
import jax.numpy as jnp
from jax import lax
from jax.experimental import pallas as pl
from jax.experimental.pallas import tpu as pltpu
from jax.sharding import Mesh
from jax.sharding import PartitionSpec as P

SAMPLE = ("sample_0", "sample_1", "sample_2")
MESH = pl.DeviceIdType.MESH
F32 = jnp.float32
BF16 = jnp.bfloat16

learn_rate = 64.0
slope_one = 0.197
cube_coef = 0.004

ROWS = 256
COLS = 1024
PH = 256
CHUNK = 64
CHUNKS = ROWS // CHUNK
BLOCKS = 2
BLOCK = ROWS // BLOCKS
PER = CHUNKS // BLOCKS
FEATS = 8
PIECE = BLOCK // FEATS
HALF = COLS // 2
SUBS = 2
SUB = HALF // SUBS
QUARTER = SUB // 4
LAST = QUARTER // 4
SMALL = 6
ALONG = (4, 3, 5, 2, 6, 1, 7)


def kernel(
    x_ref, a_ref, w_ref, b_ref, c_ref, lin_ref, sq_ref, cube_ref, y_ref, r_ref,
    grad_ref,
    xv, av, wv, bv, sv, mv, om, ev, et, ea, wm, ow, opened, zv, zbuf, psum, pack, pbuf,
    rr, gv, gbuf, xbuf, hv, hbuf,
    y_token, z_token, x_token, load_sem, in_send, in_recv, wt_send, wt_recv, pk_send, pk_recv,
    z_send, z_recv, p_send, p_recv, r_send, r_recv, g_send, g_recv, x_send, x_recv,
    h_send, h_recv, f_send, f_recv, e_send, e_recv, k_send, k_recv,
):
    party = lax.axis_index("party")
    xi = lax.axis_index("sample_0")
    hi = lax.axis_index("sample_1")
    core = lax.axis_index("sample_2")
    feat = lax.axis_index("feat")
    select = (party == 0).astype(F32)

    def at_place(p=None, x=None, h=None, c=None, f=None):
        return (
            party if p is None else p,
            xi if x is None else x,
            hi if h is None else h,
            core if c is None else c,
            feat if f is None else f,
        )

    partner = at_place(p=1 - party)
    sibling = at_place(c=1 - core)
    other_z = at_place(p=1 - party, h=lax.rem(hi + 3 + 2 * party, 4))

    def along_y(d):
        return at_place(f=lax.rem(feat + d, FEATS))

    def along_x(d):
        return at_place(x=lax.rem(xi + d, 4))

    def along_z(d):
        return at_place(h=lax.rem(hi + d, 4))

    loads = [
        pltpu.make_async_copy(src.at[0], dst, load_sem.at[i])
        for i, (src, dst) in enumerate(
            [(x_ref, xv), (a_ref, av), (w_ref, wv), (b_ref, bv)]
            + [
                (ref, sv.at[i])
                for i, ref in enumerate((c_ref, lin_ref, sq_ref, cube_ref, y_ref, r_ref))
            ]
        )
    ]
    for load in loads:
        load.start()

    near_y, near_x, near_z = [along_y(1), along_y(7)], [along_x(1), along_x(3)], [partner, other_z]
    greeted = near_z + near_y + near_x + [sibling]
    barrier = pltpu.get_barrier_semaphore()
    for place in greeted:
        pl.semaphore_signal(barrier, inc=1, device_id=place, device_id_type=MESH)

    loads[0].wait()
    loads[1].wait()
    mv[...] = (xv[...].astype(F32) - av[...].astype(F32)).astype(BF16)
    pl.semaphore_wait(barrier, len(greeted))

    def pass_on(r):
        for token, places in ((y_token, near_y), (z_token, near_z), (x_token, near_x)):
            if r < token.shape[0]:
                for place in places:
                    pl.semaphore_signal(token.at[r], inc=1, device_id=place, device_id_type=MESH)

    def hear(r):
        for token in (y_token, z_token, x_token):
            if r < token.shape[0]:
                pl.semaphore_wait(token.at[r], 2)

    sent = []

    def remote(src, dst, send, recv, place):
        copy = pltpu.make_async_remote_copy(
            src_ref=src, dst_ref=dst, send_sem=send, recv_sem=recv,
            device_id=place, device_id_type=MESH,
        )
        copy.start()
        sent.append(copy)
        return copy

    def slab(first, size):
        return pl.ds(pl.multiple_of(first, size), size)

    inputs = []
    for k in range(CHUNKS):
        rows = pl.ds(k * CHUNK, CHUNK)
        inputs.append(remote(mv.at[rows], om.at[rows], in_send.at[k], in_recv.at[k], partner))
    my_half = slab(core * HALF, HALF)
    loads[2].wait()
    loads[3].wait()
    wm[...] = (wv[...] - bv[...].astype(F32)).astype(BF16)
    weights = remote(wm.at[my_half], ow.at[my_half], wt_send.at[0], wt_recv.at[0], other_z)
    pass_on(0)

    for load in loads[4:]:
        load.wait()
    for i in range(SMALL):
        for j in range(BLOCKS):
            pack[i, pl.ds(j * PIECE, PIECE), :] = sv[i, slab(j * BLOCK + feat * PIECE, PIECE), :]
    packed = remote(pack, pbuf, pk_send.at[0], pk_recv.at[0], partner)

    ea[:, ROWS:] = av[...].T
    hear(0)
    pass_on(1)
    hear(1)
    pass_on(2)
    hear(2)
    weights.wait_recv()
    passed = remote(ow.at[my_half], ow.at[my_half], wt_send.at[1], wt_recv.at[1], sibling)
    passed.wait_recv()
    opened[...] = (wm[...].astype(F32) + ow[...].astype(F32)).astype(BF16)
    zv[...] = jnp.dot(av[...], opened[...], preferred_element_type=F32)

    def margins(k):
        rows = pl.ds(k * CHUNK, CHUNK)
        inputs[k].wait_recv()
        part = (mv[rows, :].astype(F32) + om[rows, :].astype(F32)).astype(BF16)
        ev[rows, :] = part
        both = select * jnp.dot(part, opened[...], preferred_element_type=F32)
        zv[rows, :] += both + jnp.dot(part, bv[...], preferred_element_type=F32)

    def share(j):
        copies = []
        for d in ALONG:
            rows = slab(j * BLOCK + lax.rem(feat + d, FEATS) * PIECE, PIECE)
            copies.append(
                remote(zv.at[rows], zbuf.at[j, d], z_send.at[j, d], z_recv.at[j, d], along_y(d))
            )
        return copies

    def add_up(j, copies):
        for copy in copies:
            copy.wait_recv()
        total = zv[slab(j * BLOCK + feat * PIECE, PIECE), :]
        for d in range(1, FEATS):
            total = total + zbuf[j, d]
        psum[j, 0] = total
        return remote(psum.at[j, 0], psum.at[j, 1], p_send.at[j], p_recv.at[j], partner)

    def residuals(j, copy):
        copy.wait_recv()
        own_rows = pl.ds(j * PIECE, PIECE)
        own = [pack[i, own_rows, :].astype(F32) for i in range(SMALL)]
        far = [pbuf[i, own_rows, :].astype(F32) for i in range(SMALL)]
        own_margin, far_margin = psum[j, 0] + own[0], psum[j, 1] + far[0]
        spread = (own_margin - own[1]) + (far_margin - far[1])

        def masked(s, margin, value):
            cubed = s * (spread * spread * spread) + 3.0 * (spread * spread) * value[1]
            cubed = cubed + 3.0 * spread * value[2] + value[3]
            result = 0.5 * s + slope_one * margin - cube_coef * cubed - value[4]
            return (result - value[5]).astype(BF16).astype(F32)

        both = masked(select, own_margin, own) + masked(1.0 - select, far_margin, far)
        rows = slab(j * BLOCK + feat * PIECE, PIECE)
        rr[rows, :] = both.astype(BF16)
        return [
            remote(rr.at[rows], rr.at[rows], r_send.at[j, d], r_recv.at[j, d], along_y(d))
            for d in ALONG
        ]

    def turned(j):
        rows = pl.ds(j * BLOCK, BLOCK)
        flipped = ev[rows, :].T
        et[:, rows] = flipped
        ea[:, rows] = (flipped.astype(F32) * select).astype(BF16)

    margins(0)
    margins(1)
    shared_0 = share(0)
    turned(0)
    margins(2)
    margins(3)
    shared_1 = share(1)
    summed_0 = add_up(0, shared_0)
    packed.wait_recv()
    opened_0 = residuals(0, summed_0)
    turned(1)
    gv[...] = jnp.dot(et[...], sv[SMALL - 1], preferred_element_type=F32)
    summed_1 = add_up(1, shared_1)
    opened_1 = residuals(1, summed_1)
    for copy in opened_0 + opened_1:
        copy.wait_recv()
    rr[ROWS:, :] = rr[:ROWS, :]

    def terms(first):
        rows = slab(first, SUB)
        return gv[rows, :] + jnp.dot(ea[rows, :], rr[...], preferred_element_type=F32)

    crossing = []
    for n in range(SUBS):
        their = slab((1 - core) * HALF + n * SUB, SUB)
        gv[their, :] = terms((1 - core) * HALF + n * SUB)
        crossing.append(remote(gv.at[their], gbuf.at[n], g_send.at[n], g_recv.at[n], sibling))
    for n in range(SUBS):
        gv[slab(core * HALF + n * SUB, SUB), :] = terms(core * HALF + n * SUB)

    quarters = []
    for n in range(SUBS):
        crossing[n].wait_recv()
        gbuf[n] += gv[slab(core * HALF + n * SUB, SUB), :]
        quarters.append(
            [
                remote(
                    gbuf.at[n, slab(lax.rem(xi + d, 4) * QUARTER, QUARTER)],
                    xbuf.at[n, d], x_send.at[n, d], x_recv.at[n, d], along_x(d),
                )
                for d in (2, 1, 3)
            ]
        )
    lasts = []
    for n in range(SUBS):
        for copy in quarters[n]:
            copy.wait_recv()
        total = gbuf[n, slab(xi * QUARTER, QUARTER), :]
        hv[n] = total + xbuf[n, 1] + xbuf[n, 2] + xbuf[n, 3]
        lasts.append(
            [
                remote(
                    hv.at[n, slab(lax.rem(hi + d, 4) * LAST, LAST)],
                    hbuf.at[n, d], h_send.at[n, d], h_recv.at[n, d], along_z(d),
                )
                for d in (2, 1, 3)
            ]
        )
    back_z = []
    for n in range(SUBS):
        for copy in lasts[n]:
            copy.wait_recv()
        total = hv[n, slab(hi * LAST, LAST), :]
        total = total + hbuf[n, 1] + hbuf[n, 2] + hbuf[n, 3]
        rows = slab(core * HALF + n * SUB + xi * QUARTER + hi * LAST, LAST)
        grad_ref[rows, :] = total.astype(BF16)
        back_z.append(
            [
                remote(grad_ref.at[rows], grad_ref.at[rows], f_send.at[n, d], f_recv.at[n, d], along_z(d))
                for d in (2, 1, 3)
            ]
        )
    back_x = []
    for n in range(SUBS):
        for copy in back_z[n]:
            copy.wait_recv()
        rows = slab(core * HALF + n * SUB + xi * QUARTER, QUARTER)
        back_x.append(
            [
                remote(grad_ref.at[rows], grad_ref.at[rows], e_send.at[n, d], e_recv.at[n, d], along_x(d))
                for d in (2, 1, 3)
            ]
        )
    back_core = []
    for n in range(SUBS):
        for copy in back_x[n]:
            copy.wait_recv()
        rows = slab(core * HALF + n * SUB, SUB)
        back_core.append(
            remote(grad_ref.at[rows], grad_ref.at[rows], k_send.at[n], k_recv.at[n], sibling)
        )
    for copy in back_core:
        copy.wait_recv()
    for copy in sent:
        copy.wait_send()


def gradient(x, a, w, b, c, lin, sq, cube, y, r):
    dma = pltpu.SemaphoreType.DMA
    return pl.pallas_call(
        kernel,
        out_shape=jax.ShapeDtypeStruct((COLS, PH), BF16),
        in_specs=[pl.BlockSpec(memory_space=pltpu.HBM)] * 10,
        out_specs=pl.BlockSpec(memory_space=pltpu.VMEM),
        scratch_shapes=[
            pltpu.VMEM((ROWS, COLS), BF16),
            pltpu.VMEM((ROWS, COLS), BF16),
            pltpu.VMEM((COLS, PH), F32),
            pltpu.VMEM((COLS, PH), BF16),
            pltpu.VMEM((SMALL, ROWS, PH), BF16),
            pltpu.VMEM((ROWS, COLS), BF16),
            pltpu.VMEM((ROWS, COLS), BF16),
            pltpu.VMEM((ROWS, COLS), BF16),
            pltpu.VMEM((COLS, ROWS), BF16),
            pltpu.VMEM((COLS, 2 * ROWS), BF16),
            pltpu.VMEM((COLS, PH), BF16),
            pltpu.VMEM((COLS, PH), BF16),
            pltpu.VMEM((COLS, PH), BF16),
            pltpu.VMEM((ROWS, PH), F32),
            pltpu.VMEM((BLOCKS, FEATS, PIECE, PH), F32),
            pltpu.VMEM((BLOCKS, 2, PIECE, PH), F32),
            pltpu.VMEM((SMALL, BLOCKS * PIECE, PH), BF16),
            pltpu.VMEM((SMALL, BLOCKS * PIECE, PH), BF16),
            pltpu.VMEM((2 * ROWS, PH), BF16),
            pltpu.VMEM((COLS, PH), F32),
            pltpu.VMEM((SUBS, SUB, PH), F32),
            pltpu.VMEM((SUBS, 4, QUARTER, PH), F32),
            pltpu.VMEM((SUBS, QUARTER, PH), F32),
            pltpu.VMEM((SUBS, 4, LAST, PH), F32),
            pltpu.SemaphoreType.REGULAR((3,)),
            pltpu.SemaphoreType.REGULAR((3,)),
            pltpu.SemaphoreType.REGULAR((1,)),
            dma((10,)),
            dma((CHUNKS,)), dma((CHUNKS,)),
            dma((2,)), dma((2,)),
            dma((1,)), dma((1,)),
            dma((BLOCKS, FEATS)), dma((BLOCKS, FEATS)),
            dma((BLOCKS,)), dma((BLOCKS,)),
            dma((BLOCKS, FEATS)), dma((BLOCKS, FEATS)),
            dma((SUBS,)), dma((SUBS,)),
            dma((SUBS, 4)), dma((SUBS, 4)),
            dma((SUBS, 4)), dma((SUBS, 4)),
            dma((SUBS, 4)), dma((SUBS, 4)),
            dma((SUBS, 4)), dma((SUBS, 4)),
            dma((SUBS,)), dma((SUBS,)),
        ],
        compiler_params=pltpu.CompilerParams(
            collective_id=0, has_side_effects=True, vmem_limit_bytes=60 * 2**20
        ),
        cost_estimate=pl.CostEstimate(
            flops=12 * ROWS * COLS * PH, bytes_accessed=5 * 2**20, transcendentals=0
        ),
    )(x, a, w, b, c, lin, sq, cube, y, r)


def shards(x, a, w, b, c, lin, sq, cube, y, r, grad_product):
    grad = gradient(x, a, w, b, c, lin, sq, cube, y, r)
    samples = x.shape[1] * lax.axis_size(SAMPLE)
    whole = grad.astype(F32) + grad_product[0].astype(F32)
    return (w[0] - learn_rate / samples * whole)[None]


def solution(mesh):
    torus = Mesh(
        mesh.devices.reshape(mesh.shape["party"], 4, 4, 2, mesh.shape["feat"]),
        ("party", "sample_0", "sample_1", "sample_2", "feat"),
    )
    return jax.shard_map(
        shards,
        mesh=torus,
        in_specs=(
            P("party", SAMPLE, "feat"),
            P("party", SAMPLE, "feat"),
            P("party", "feat", None),
            P("party", "feat", None),
            P("party", SAMPLE, None),
            P("party", SAMPLE, None),
            P("party", SAMPLE, None),
            P("party", SAMPLE, None),
            P("party", SAMPLE, None),
            P("party", SAMPLE, None),
            P("party", "feat", None),
        ),
        out_specs=P("party", "feat", None),
        check_vma=False,
    )
```

time: 81.7 us -> 68.4 us (0.84)
  local copies, waits for them, and re-layouts: 9.77 us -> 0.01 us
  Pallas kernels: 70.4 us -> 66.1 us
  other arithmetic: 1.14 us -> 2.18 us
    unnamed x22 -> x4, local copies, waits for them, and re-layouts: 9.77 us -> 0.01 us
    pallas_call x1, Pallas kernels: 70.4 us -> 66.1 us  [gradient(): pl.pallas_call(kernel, out_shape=jax.ShapeDtypeStruct((COLS, PH), BF16),...]
    broadcast_in_dim x1, other arithmetic: 1.14 us -> 2.18 us  [shards(): return (w[0] - learn_rate / samples * whole)[None]]
where the time goes in v2:
time: 68.4 us; the launch traced here: 68.3 us
  Pallas kernels  66.1 us (97%)
  other arithmetic  2.18 us (3%)
    pallas_call x1, Pallas kernels, gradient(): pl.pallas_call(kernel, out_shape=jax.ShapeDtypeStruct((COLS, PH), BF16),...  66.1 us
    broadcast_in_dim x1, other arithmetic, shards(): return (w[0] - learn_rate / samples * whole)[None]  2.18 us

profile of v2, /device:TPU:1, one launch (start us, length us, event | category | flops | bytes accessed | tf_op | source)
XLA Modules:
  0.0 68.3 jit_solution(3815510405086190799)
XLA Ops:
  0.0 0.0 copy-start
  0.0 0.0 copy-start.1
  0.0 66.1 %shard_map.109 = bf16[1024,256]{1,0:T(8,128)(2,1)} custom-call(bf16[1,256,1024]{2,1,0:T(8,128)(2,1)} %x_ref.1, bf16[1,256,1024]{2,1,0:T(8,128)(2,1)} %a_ref.1, f32[1,1024,256]{2,1,0:T(8,128)} %w_ref.1, bf16[1,1024,256]{2,1,0:T(8,128)(2,1)} %b_ref.1, bf16[1,256,256]{2,1,0:T(8,128)(2,1)} %c_ref.1, bf16[1,256,256]{2,1,0:T(8,128)(2,1)} %lin_ref.1, ...), custom_call_target="tpu_custom_call" | custom-call | flops 805306368 | bytes 5242880 | tf_op jit(solution)/shard_map/pallas_call | solution.py:307
  66.1 0.0 copy-done
  66.1 0.0 copy-done.1
  66.1 2.2 %fusion.2 = f32[1,1024,256]{2,1,0:T(8,128)} fusion(f32[1,1024,256]{2,1,0:T(8,128)S(1)} %copy-done, bf16[1024,256]{1,0:T(8,128)(2,1)} %shard_map.109, bf16[1,1024,256]{2,1,0:T(8,128)(2,1)S(1)} %copy-done.1), kind=kLoop, calls=%fused_computation.3 | loop fusion | flops 1310720 | bytes 3145728 | tf_op jit(solution)/shard_map/broadcast_in_dim | solution.py:367
Async XLA Ops:
  0.0 66.1 %copy-start = (f32[1,1024,256]{2,1,0:T(8,128)S(1)}, f32[1,1024,256]{2,1,0:T(8,128)}, u32[]{:S(2)}) copy-start(f32[1,1024,256]{2,1,0:T(8,128)} %w_ref.1) | copy-start | bytes 3145732
  0.0 66.1 %copy-start.1 = (bf16[1,1024,256]{2,1,0:T(8,128)(2,1)S(1)}, bf16[1,1024,256]{2,1,0:T(8,128)(2,1)}, u32[]{:S(2)}) copy-start(bf16[1,1024,256]{2,1,0:T(8,128)(2,1)} %param.21) | copy-start | bytes 1572868

commit v3 on v2

--- a/solution.py
+++ b/solution.py
@@ -32,13 +32,35 @@
 LAST = QUARTER // 4
 SMALL = 6
 ALONG = (4, 3, 5, 2, 6, 1, 7)
+MIDDLE = 120.0
+GRADIENT = (-22.0, 384.0)
+MARGIN = (-14.0, 960.0)
+
+
+def coded(value, span):
+    least, step = span
+    level = jnp.log2(jnp.maximum(jnp.abs(value), 2.0**least)) - least
+    level = jnp.floor(level * step + 0.5)
+    high = jnp.floor(level * (1 / 128))
+    code = jnp.exp2(high - MIDDLE) * (1.0 + (level - 128.0 * high) * (1 / 128))
+    return jnp.where(value < 0, -code, code).astype(BF16)
+
+
+def decoded(code, span):
+    least, step = span
+    code = code.astype(F32)
+    size = jnp.abs(code)
+    high = jnp.floor(jnp.log2(size) + 0.003)
+    low = size * jnp.exp2(-high) - 1.0
+    value = jnp.exp2((low + (high + MIDDLE)) * (128 / step) + least)
+    return jnp.where(code < 0, -value, value)
 
 
 def kernel(
     x_ref, a_ref, w_ref, b_ref, c_ref, lin_ref, sq_ref, cube_ref, y_ref, r_ref,
     grad_ref,
-    xv, av, wv, bv, sv, mv, om, ev, et, ea, wm, ow, opened, zv, zbuf, psum, pack, pbuf,
-    rr, gv, gbuf, xbuf, hv, hbuf,
+    xv, av, wv, bv, sv, mv, om, ev, et, ea, wm, ow, opened, zv, zc, zbuf, psum, pack, pbuf,
+    rr, gv, gbuf, gc, xbuf, hv, hc, hbuf, back,
     y_token, z_token, x_token, load_sem, in_send, in_recv, wt_send, wt_recv, pk_send, pk_recv,
     z_send, z_recv, p_send, p_recv, r_send, r_recv, g_send, g_recv, x_send, x_recv,
     h_send, h_recv, f_send, f_recv, e_send, e_recv, k_send, k_recv,
@@ -72,6 +94,9 @@
     def along_z(d):
         return at_place(h=lax.rem(hi + d, 4))
 
+    near_y, near_x, near_z = [along_y(1), along_y(7)], [along_x(1), along_x(3)], [partner, other_z]
+    greeted = near_z + [sibling] + near_y + near_x
+    barrier = pltpu.get_barrier_semaphore()
     loads = [
         pltpu.make_async_copy(src.at[0], dst, load_sem.at[i])
         for i, (src, dst) in enumerate(
@@ -82,14 +107,12 @@
             ]
         )
     ]
-    for load in loads:
-        load.start()
-
-    near_y, near_x, near_z = [along_y(1), along_y(7)], [along_x(1), along_x(3)], [partner, other_z]
-    greeted = near_z + near_y + near_x + [sibling]
-    barrier = pltpu.get_barrier_semaphore()
+    loads[0].start()
+    loads[1].start()
     for place in greeted:
         pl.semaphore_signal(barrier, inc=1, device_id=place, device_id_type=MESH)
+    for load in loads[2:]:
+        load.start()
 
     loads[0].wait()
     loads[1].wait()
@@ -157,14 +180,16 @@
         part = (mv[rows, :].astype(F32) + om[rows, :].astype(F32)).astype(BF16)
         ev[rows, :] = part
         both = select * jnp.dot(part, opened[...], preferred_element_type=F32)
-        zv[rows, :] += both + jnp.dot(part, bv[...], preferred_element_type=F32)
+        total = zv[rows, :] + both + jnp.dot(part, bv[...], preferred_element_type=F32)
+        zv[rows, :] = total
+        zc[rows, :] = coded(total, MARGIN)
 
     def share(j):
         copies = []
         for d in ALONG:
             rows = slab(j * BLOCK + lax.rem(feat + d, FEATS) * PIECE, PIECE)
             copies.append(
-                remote(zv.at[rows], zbuf.at[j, d], z_send.at[j, d], z_recv.at[j, d], along_y(d))
+                remote(zc.at[rows], zbuf.at[j, d], z_send.at[j, d], z_recv.at[j, d], along_y(d))
             )
         return copies
 
@@ -173,7 +198,7 @@
             copy.wait_recv()
         total = zv[slab(j * BLOCK + feat * PIECE, PIECE), :]
         for d in range(1, FEATS):
-            total = total + zbuf[j, d]
+            total = total + decoded(zbuf[j, d], MARGIN)
         psum[j, 0] = total
         return remote(psum.at[j, 0], psum.at[j, 1], p_send.at[j], p_recv.at[j], partner)
 
@@ -238,11 +263,13 @@
     quarters = []
     for n in range(SUBS):
         crossing[n].wait_recv()
-        gbuf[n] += gv[slab(core * HALF + n * SUB, SUB), :]
+        total = gbuf[n] + gv[slab(core * HALF + n * SUB, SUB), :]
+        gbuf[n] = total
+        gc[n] = coded(total, GRADIENT)
         quarters.append(
             [
                 remote(
-                    gbuf.at[n, slab(lax.rem(xi + d, 4) * QUARTER, QUARTER)],
+                    gc.at[n, slab(lax.rem(xi + d, 4) * QUARTER, QUARTER)],
                     xbuf.at[n, d], x_send.at[n, d], x_recv.at[n, d], along_x(d),
                 )
                 for d in (2, 1, 3)
@@ -253,11 +280,13 @@
         for copy in quarters[n]:
             copy.wait_recv()
         total = gbuf[n, slab(xi * QUARTER, QUARTER), :]
-        hv[n] = total + xbuf[n, 1] + xbuf[n, 2] + xbuf[n, 3]
+        total = total + decoded(xbuf[n, 1], GRADIENT) + decoded(xbuf[n, 2], GRADIENT) + decoded(xbuf[n, 3], GRADIENT)
+        hv[n] = total
+        hc[n] = coded(total, GRADIENT)
         lasts.append(
             [
                 remote(
-                    hv.at[n, slab(lax.rem(hi + d, 4) * LAST, LAST)],
+                    hc.at[n, slab(lax.rem(hi + d, 4) * LAST, LAST)],
                     hbuf.at[n, d], h_send.at[n, d], h_recv.at[n, d], along_z(d),
                 )
                 for d in (2, 1, 3)
@@ -268,12 +297,12 @@
         for copy in lasts[n]:
             copy.wait_recv()
         total = hv[n, slab(hi * LAST, LAST), :]
-        total = total + hbuf[n, 1] + hbuf[n, 2] + hbuf[n, 3]
+        total = total + decoded(hbuf[n, 1], GRADIENT) + decoded(hbuf[n, 2], GRADIENT) + decoded(hbuf[n, 3], GRADIENT)
         rows = slab(core * HALF + n * SUB + xi * QUARTER + hi * LAST, LAST)
-        grad_ref[rows, :] = total.astype(BF16)
+        back[rows, :] = coded(total, GRADIENT)
         back_z.append(
             [
-                remote(grad_ref.at[rows], grad_ref.at[rows], f_send.at[n, d], f_recv.at[n, d], along_z(d))
+                remote(back.at[rows], back.at[rows], f_send.at[n, d], f_recv.at[n, d], along_z(d))
                 for d in (2, 1, 3)
             ]
         )
@@ -284,7 +313,7 @@
         rows = slab(core * HALF + n * SUB + xi * QUARTER, QUARTER)
         back_x.append(
             [
-                remote(grad_ref.at[rows], grad_ref.at[rows], e_send.at[n, d], e_recv.at[n, d], along_x(d))
+                remote(back.at[rows], back.at[rows], e_send.at[n, d], e_recv.at[n, d], along_x(d))
                 for d in (2, 1, 3)
             ]
         )
@@ -294,10 +323,15 @@
             copy.wait_recv()
         rows = slab(core * HALF + n * SUB, SUB)
         back_core.append(
-            remote(grad_ref.at[rows], grad_ref.at[rows], k_send.at[n], k_recv.at[n], sibling)
-        )
-    for copy in back_core:
-        copy.wait_recv()
+            remote(back.at[rows], back.at[rows], k_send.at[n], k_recv.at[n], sibling)
+        )
+    for n in range(SUBS):
+        rows = slab(core * HALF + n * SUB, SUB)
+        grad_ref[rows, :] = decoded(back[rows, :], GRADIENT)
+    for n in range(SUBS):
+        back_core[n].wait_recv()
+        rows = slab((1 - core) * HALF + n * SUB, SUB)
+        grad_ref[rows, :] = decoded(back[rows, :], GRADIENT)
     for copy in sent:
         copy.wait_send()
 
@@ -306,7 +340,7 @@
     dma = pltpu.SemaphoreType.DMA
     return pl.pallas_call(
         kernel,
-        out_shape=jax.ShapeDtypeStruct((COLS, PH), BF16),
+        out_shape=pltpu.VMEM((COLS, PH), F32),
         in_specs=[pl.BlockSpec(memory_space=pltpu.HBM)] * 10,
         out_specs=pl.BlockSpec(memory_space=pltpu.VMEM),
         scratch_shapes=[
@@ -324,16 +358,20 @@
             pltpu.VMEM((COLS, PH), BF16),
             pltpu.VMEM((COLS, PH), BF16),
             pltpu.VMEM((ROWS, PH), F32),
-            pltpu.VMEM((BLOCKS, FEATS, PIECE, PH), F32),
+            pltpu.VMEM((ROWS, PH), BF16),
+            pltpu.VMEM((BLOCKS, FEATS, PIECE, PH), BF16),
             pltpu.VMEM((BLOCKS, 2, PIECE, PH), F32),
             pltpu.VMEM((SMALL, BLOCKS * PIECE, PH), BF16),
             pltpu.VMEM((SMALL, BLOCKS * PIECE, PH), BF16),
             pltpu.VMEM((2 * ROWS, PH), BF16),
             pltpu.VMEM((COLS, PH), F32),
             pltpu.VMEM((SUBS, SUB, PH), F32),
-            pltpu.VMEM((SUBS, 4, QUARTER, PH), F32),
+            pltpu.VMEM((SUBS, SUB, PH), BF16),
+            pltpu.VMEM((SUBS, 4, QUARTER, PH), BF16),
             pltpu.VMEM((SUBS, QUARTER, PH), F32),
-            pltpu.VMEM((SUBS, 4, LAST, PH), F32),
+            pltpu.VMEM((SUBS, QUARTER, PH), BF16),
+            pltpu.VMEM((SUBS, 4, LAST, PH), BF16),
+            pltpu.VMEM((COLS, PH), BF16),
             pltpu.SemaphoreType.REGULAR((3,)),
             pltpu.SemaphoreType.REGULAR((3,)),
             pltpu.SemaphoreType.REGULAR((1,)),
@@ -363,7 +401,7 @@
 def shards(x, a, w, b, c, lin, sq, cube, y, r, grad_product):
     grad = gradient(x, a, w, b, c, lin, sq, cube, y, r)
     samples = x.shape[1] * lax.axis_size(SAMPLE)
-    whole = grad.astype(F32) + grad_product[0].astype(F32)
+    whole = grad + grad_product[0].astype(F32)
     return (w[0] - learn_rate / samples * whole)[None]
 
 

time: 68.4 us -> 63.5 us (0.928)
  Pallas kernels: 66.1 us -> 62.3 us
  other arithmetic: 2.18 us -> 1.14 us
    pallas_call x1, Pallas kernels: 66.1 us -> 62.3 us  [gradient(): pl.pallas_call(kernel, out_shape=pltpu.VMEM((COLS, PH), F32), in_specs=[p...]
    broadcast_in_dim x1, other arithmetic: 2.18 us -> 1.14 us  [shards(): return (w[0] - learn_rate / samples * whole)[None]]
where the time goes in v3:
time: 63.5 us; the launch traced here: 63.4 us
  Pallas kernels  62.3 us (98%)
  other arithmetic  1.14 us (2%)
    pallas_call x1, Pallas kernels, gradient(): pl.pallas_call(kernel, out_shape=pltpu.VMEM((COLS, PH), F32), in_specs=[p...  62.3 us

profile of v3, /device:TPU:1, one launch (start us, length us, event | category | flops | bytes accessed | tf_op | source)
XLA Modules:
  0.0 63.4 jit_solution(12663623502608032614)
XLA Ops:
  0.0 0.0 copy-start
  0.0 0.0 copy-start.1
  0.0 62.3 %shard_map.109 = f32[1024,256]{1,0:T(8,128)S(1)} custom-call(bf16[1,256,1024]{2,1,0:T(8,128)(2,1)} %x_ref.1, bf16[1,256,1024]{2,1,0:T(8,128)(2,1)} %a_ref.1, f32[1,1024,256]{2,1,0:T(8,128)} %w_ref.1, bf16[1,1024,256]{2,1,0:T(8,128)(2,1)} %b_ref.1, bf16[1,256,256]{2,1,0:T(8,128)(2,1)} %c_ref.1, bf16[1,256,256]{2,1,0:T(8,128)(2,1)} %lin_ref.1, ...), custom_call_target="tpu_custom_call" | custom-call | flops 805306368 | bytes 5242880 | tf_op jit(solution)/shard_map/pallas_call | solution.py:341
  62.3 0.0 copy-done
  62.3 0.0 copy-done.1
  62.3 1.1 %fusion.2 = f32[1,1024,256]{2,1,0:T(8,128)} fusion(f32[1024,256]{1,0:T(8,128)S(1)} %shard_map.109, f32[1,1024,256]{2,1,0:T(8,128)S(1)} %copy-done, bf16[1,1024,256]{2,1,0:T(8,128)(2,1)S(1)} %copy-done.1), kind=kLoop, calls=%fused_computation.3 | loop fusion | flops 1048576 | bytes 3670016 | tf_op jit(solution)/shard_map/broadcast_in_dim | solution.py:405
Async XLA Ops:
  0.0 62.3 %copy-start = (f32[1,1024,256]{2,1,0:T(8,128)S(1)}, f32[1,1024,256]{2,1,0:T(8,128)}, u32[]{:S(2)}) copy-start(f32[1,1024,256]{2,1,0:T(8,128)} %w_ref.1) | copy-start | bytes 3145732
  0.0 62.3 %copy-start.1 = (bf16[1,1024,256]{2,1,0:T(8,128)(2,1)S(1)}, bf16[1,1024,256]{2,1,0:T(8,128)(2,1)}, u32[]{:S(2)}) copy-start(bf16[1,1024,256]{2,1,0:T(8,128)(2,1)} %param.21) | copy-start | bytes 1572868

commit v4 on v3

--- a/solution.py
+++ b/solution.py
@@ -26,10 +26,9 @@
 FEATS = 8
 PIECE = BLOCK // FEATS
 HALF = COLS // 2
-SUBS = 2
+SUBS = 4
 SUB = HALF // SUBS
 QUARTER = SUB // 4
-LAST = QUARTER // 4
 SMALL = 6
 ALONG = (4, 3, 5, 2, 6, 1, 7)
 MIDDLE = 120.0
@@ -60,10 +59,10 @@
     x_ref, a_ref, w_ref, b_ref, c_ref, lin_ref, sq_ref, cube_ref, y_ref, r_ref,
     grad_ref,
     xv, av, wv, bv, sv, mv, om, ev, et, ea, wm, ow, opened, zv, zc, zbuf, psum, pack, pbuf,
-    rr, gv, gbuf, gc, xbuf, hv, hc, hbuf, back,
-    y_token, z_token, x_token, load_sem, in_send, in_recv, wt_send, wt_recv, pk_send, pk_recv,
+    rr, gv, gbuf, gc, xbuf, hbuf, back,
+    y_token, z_token, x_token, load_sem, first_sem, in_send, in_recv, wt_send, wt_recv, pk_send, pk_recv,
     z_send, z_recv, p_send, p_recv, r_send, r_recv, g_send, g_recv, x_send, x_recv,
-    h_send, h_recv, f_send, f_recv, e_send, e_recv, k_send, k_recv,
+    h_send, h_recv, e_send, e_recv, k_send, k_recv,
 ):
     party = lax.axis_index("party")
     xi = lax.axis_index("sample_0")
@@ -100,23 +99,34 @@
     loads = [
         pltpu.make_async_copy(src.at[0], dst, load_sem.at[i])
         for i, (src, dst) in enumerate(
-            [(x_ref, xv), (a_ref, av), (w_ref, wv), (b_ref, bv)]
+            [(w_ref, wv), (b_ref, bv)]
             + [
                 (ref, sv.at[i])
                 for i, ref in enumerate((c_ref, lin_ref, sq_ref, cube_ref, y_ref, r_ref))
             ]
         )
     ]
-    loads[0].start()
-    loads[1].start()
+    first_loads = []
+    for k in range(CHUNKS):
+        rows = pl.ds(k * CHUNK, CHUNK)
+        for i, (src, dst) in enumerate([(x_ref, xv), (a_ref, av)]):
+            first_loads.append(
+                pltpu.make_async_copy(src.at[0, rows], dst.at[rows], first_sem.at[k, i])
+            )
+            first_loads[-1].start()
     for place in greeted:
         pl.semaphore_signal(barrier, inc=1, device_id=place, device_id_type=MESH)
-    for load in loads[2:]:
+    for load in loads:
         load.start()
 
-    loads[0].wait()
-    loads[1].wait()
-    mv[...] = (xv[...].astype(F32) - av[...].astype(F32)).astype(BF16)
+
+    def masked_chunk(k):
+        first_loads[2 * k].wait()
+        first_loads[2 * k + 1].wait()
+        rows = pl.ds(k * CHUNK, CHUNK)
+        mv[rows, :] = (xv[rows, :].astype(F32) - av[rows, :].astype(F32)).astype(BF16)
+
+    masked_chunk(0)
     pl.semaphore_wait(barrier, len(greeted))
 
     def pass_on(r):
@@ -146,16 +156,18 @@
 
     inputs = []
     for k in range(CHUNKS):
+        if k > 0:
+            masked_chunk(k)
         rows = pl.ds(k * CHUNK, CHUNK)
         inputs.append(remote(mv.at[rows], om.at[rows], in_send.at[k], in_recv.at[k], partner))
     my_half = slab(core * HALF, HALF)
-    loads[2].wait()
-    loads[3].wait()
+    loads[0].wait()
+    loads[1].wait()
     wm[...] = (wv[...] - bv[...].astype(F32)).astype(BF16)
     weights = remote(wm.at[my_half], ow.at[my_half], wt_send.at[0], wt_recv.at[0], other_z)
     pass_on(0)
 
-    for load in loads[4:]:
+    for load in loads[2:]:
         load.wait()
     for i in range(SMALL):
         for j in range(BLOCKS):
@@ -280,37 +292,23 @@
         for copy in quarters[n]:
             copy.wait_recv()
         total = gbuf[n, slab(xi * QUARTER, QUARTER), :]
-        total = total + decoded(xbuf[n, 1], GRADIENT) + decoded(xbuf[n, 2], GRADIENT) + decoded(xbuf[n, 3], GRADIENT)
-        hv[n] = total
-        hc[n] = coded(total, GRADIENT)
+        for d in (1, 2, 3):
+            total = total + decoded(xbuf[n, d], GRADIENT)
+        hbuf[n, hi] = coded(total, GRADIENT)
         lasts.append(
             [
-                remote(
-                    hc.at[n, slab(lax.rem(hi + d, 4) * LAST, LAST)],
-                    hbuf.at[n, d], h_send.at[n, d], h_recv.at[n, d], along_z(d),
-                )
+                remote(hbuf.at[n, hi], hbuf.at[n, hi], h_send.at[n, d], h_recv.at[n, d], along_z(d))
                 for d in (2, 1, 3)
             ]
         )
-    back_z = []
+    back_x = []
     for n in range(SUBS):
         for copy in lasts[n]:
             copy.wait_recv()
-        total = hv[n, slab(hi * LAST, LAST), :]
-        total = total + decoded(hbuf[n, 1], GRADIENT) + decoded(hbuf[n, 2], GRADIENT) + decoded(hbuf[n, 3], GRADIENT)
-        rows = slab(core * HALF + n * SUB + xi * QUARTER + hi * LAST, LAST)
+        total = decoded(hbuf[n, 0], GRADIENT) + decoded(hbuf[n, 1], GRADIENT)
+        total = total + (decoded(hbuf[n, 2], GRADIENT) + decoded(hbuf[n, 3], GRADIENT))
+        rows = slab(core * HALF + n * SUB + xi * QUARTER, QUARTER)
         back[rows, :] = coded(total, GRADIENT)
-        back_z.append(
-            [
-                remote(back.at[rows], back.at[rows], f_send.at[n, d], f_recv.at[n, d], along_z(d))
-                for d in (2, 1, 3)
-            ]
-        )
-    back_x = []
-    for n in range(SUBS):
-        for copy in back_z[n]:
-            copy.wait_recv()
-        rows = slab(core * HALF + n * SUB + xi * QUARTER, QUARTER)
         back_x.append(
             [
                 remote(back.at[rows], back.at[rows], e_send.at[n, d], e_recv.at[n, d], along_x(d))
@@ -368,14 +366,13 @@
             pltpu.VMEM((SUBS, SUB, PH), F32),
             pltpu.VMEM((SUBS, SUB, PH), BF16),
             pltpu.VMEM((SUBS, 4, QUARTER, PH), BF16),
-            pltpu.VMEM((SUBS, QUARTER, PH), F32),
-            pltpu.VMEM((SUBS, QUARTER, PH), BF16),
-            pltpu.VMEM((SUBS, 4, LAST, PH), BF16),
+            pltpu.VMEM((SUBS, 4, QUARTER, PH), BF16),
             pltpu.VMEM((COLS, PH), BF16),
             pltpu.SemaphoreType.REGULAR((3,)),
             pltpu.SemaphoreType.REGULAR((3,)),
             pltpu.SemaphoreType.REGULAR((1,)),
-            dma((10,)),
+            dma((8,)),
+            dma((CHUNKS, 2)),
             dma((CHUNKS,)), dma((CHUNKS,)),
             dma((2,)), dma((2,)),
             dma((1,)), dma((1,)),
@@ -383,7 +380,6 @@
             dma((BLOCKS,)), dma((BLOCKS,)),
             dma((BLOCKS, FEATS)), dma((BLOCKS, FEATS)),
             dma((SUBS,)), dma((SUBS,)),
-            dma((SUBS, 4)), dma((SUBS, 4)),
             dma((SUBS, 4)), dma((SUBS, 4)),
             dma((SUBS, 4)), dma((SUBS, 4)),
             dma((SUBS, 4)), dma((SUBS, 4)),

time: 63.5 us -> 61.2 us (0.964)
  Pallas kernels: 62.3 us -> 59.9 us
    pallas_call x1, Pallas kernels: 62.3 us -> 59.9 us  [gradient(): pl.pallas_call(kernel, out_shape=pltpu.VMEM((COLS, PH), F32), in_specs=[p...]
where the time goes in v4:
time: 61.2 us; the launch traced here: 61.1 us
  Pallas kernels  59.9 us (98%)
  other arithmetic  1.14 us (2%)
    pallas_call x1, Pallas kernels, gradient(): pl.pallas_call(kernel, out_shape=pltpu.VMEM((COLS, PH), F32), in_specs=[p...  59.9 us

profile of v4, /device:TPU:1, one launch (start us, length us, event | category | flops | bytes accessed | tf_op | source)
XLA Modules:
  0.0 61.1 jit_solution(6588781463223234091)
XLA Ops:
  0.0 0.0 copy-start
  0.0 0.0 copy-start.1
  0.0 59.9 %shard_map.109 = f32[1024,256]{1,0:T(8,128)S(1)} custom-call(bf16[1,256,1024]{2,1,0:T(8,128)(2,1)} %x_ref.1, bf16[1,256,1024]{2,1,0:T(8,128)(2,1)} %a_ref.1, f32[1,1024,256]{2,1,0:T(8,128)} %w_ref.1, bf16[1,1024,256]{2,1,0:T(8,128)(2,1)} %b_ref.1, bf16[1,256,256]{2,1,0:T(8,128)(2,1)} %c_ref.1, bf16[1,256,256]{2,1,0:T(8,128)(2,1)} %lin_ref.1, ...), custom_call_target="tpu_custom_call" | custom-call | flops 805306368 | bytes 5242880 | tf_op jit(solution)/shard_map/pallas_call | solution.py:339
  59.9 0.0 copy-done
  59.9 0.0 copy-done.1
  59.9 1.1 %fusion.2 = f32[1,1024,256]{2,1,0:T(8,128)} fusion(f32[1024,256]{1,0:T(8,128)S(1)} %shard_map.109, f32[1,1024,256]{2,1,0:T(8,128)S(1)} %copy-done, bf16[1,1024,256]{2,1,0:T(8,128)(2,1)S(1)} %copy-done.1), kind=kLoop, calls=%fused_computation.3 | loop fusion | flops 1048576 | bytes 3670016 | tf_op jit(solution)/shard_map/broadcast_in_dim | solution.py:401
Async XLA Ops:
  0.0 59.9 %copy-start = (f32[1,1024,256]{2,1,0:T(8,128)S(1)}, f32[1,1024,256]{2,1,0:T(8,128)}, u32[]{:S(2)}) copy-start(f32[1,1024,256]{2,1,0:T(8,128)} %w_ref.1) | copy-start | bytes 3145732
  0.0 59.9 %copy-start.1 = (bf16[1,1024,256]{2,1,0:T(8,128)(2,1)S(1)}, bf16[1,1024,256]{2,1,0:T(8,128)(2,1)}, u32[]{:S(2)}) copy-start(bf16[1,1024,256]{2,1,0:T(8,128)(2,1)} %param.21) | copy-start | bytes 1572868

commit v5 on v4

--- a/solution.py
+++ b/solution.py
@@ -1,3 +1,5 @@
+import functools
+
 import jax
 import jax.numpy as jnp
 from jax import lax
@@ -56,9 +58,10 @@
 
 
 def kernel(
-    x_ref, a_ref, w_ref, b_ref, c_ref, lin_ref, sq_ref, cube_ref, y_ref, r_ref,
-    grad_ref,
-    xv, av, wv, bv, sv, mv, om, ev, et, ea, wm, ow, opened, zv, zc, zbuf, psum, pack, pbuf,
+    samples,
+    x_ref, a_ref, w_ref, b_ref, c_ref, lin_ref, sq_ref, cube_ref, y_ref, r_ref, p_ref,
+    new_ref,
+    xv, av, wv, bv, pv, sv, mv, om, ev, et, ea, wm, ow, opened, zv, zc, zbuf, psum, pack, pbuf,
     rr, gv, gbuf, gc, xbuf, hbuf, back,
     y_token, z_token, x_token, load_sem, first_sem, in_send, in_recv, wt_send, wt_recv, pk_send, pk_recv,
     z_send, z_recv, p_send, p_recv, r_send, r_recv, g_send, g_recv, x_send, x_recv,
@@ -169,6 +172,8 @@
 
     for load in loads[2:]:
         load.wait()
+    load_p = pltpu.make_async_copy(p_ref.at[0], pv, load_sem.at[8])
+    load_p.start()
     for i in range(SMALL):
         for j in range(BLOCKS):
             pack[i, pl.ds(j * PIECE, PIECE), :] = sv[i, slab(j * BLOCK + feat * PIECE, PIECE), :]
@@ -264,16 +269,17 @@
         rows = slab(first, SUB)
         return gv[rows, :] + jnp.dot(ea[rows, :], rr[...], preferred_element_type=F32)
 
-    crossing = []
-    for n in range(SUBS):
-        their = slab((1 - core) * HALF + n * SUB, SUB)
-        gv[their, :] = terms((1 - core) * HALF + n * SUB)
-        crossing.append(remote(gv.at[their], gbuf.at[n], g_send.at[n], g_recv.at[n], sibling))
-    for n in range(SUBS):
+    crossing, quarters = [], []
+
+    def cross(n):
+        rows = slab((1 - core) * HALF + n * SUB, SUB)
+        gv[rows, :] = terms((1 - core) * HALF + n * SUB)
+        crossing.append(remote(gv.at[rows], gbuf.at[n], g_send.at[n], g_recv.at[n], sibling))
+
+    def keep(n):
         gv[slab(core * HALF + n * SUB, SUB), :] = terms(core * HALF + n * SUB)
 
-    quarters = []
-    for n in range(SUBS):
+    def over_x(n):
         crossing[n].wait_recv()
         total = gbuf[n] + gv[slab(core * HALF + n * SUB, SUB), :]
         gbuf[n] = total
@@ -287,6 +293,13 @@
                 for d in (2, 1, 3)
             ]
         )
+
+    for step, n in (
+        (cross, 0), (cross, 1), (keep, 0), (cross, 2), (keep, 1), (over_x, 0), (cross, 3),
+        (keep, 2), (over_x, 1), (keep, 3), (over_x, 2), (over_x, 3),
+    ):
+        step(n)
+
     lasts = []
     for n in range(SUBS):
         for copy in quarters[n]:
@@ -315,6 +328,12 @@
                 for d in (2, 1, 3)
             ]
         )
+    def update(first):
+        rows = slab(first, SUB)
+        whole = decoded(back[rows, :], GRADIENT) + pv[rows, :].astype(F32)
+        new_ref[rows, :] = wv[rows, :] - learn_rate / samples * whole
+
+    load_p.wait()
     back_core = []
     for n in range(SUBS):
         for copy in back_x[n]:
@@ -323,28 +342,26 @@
         back_core.append(
             remote(back.at[rows], back.at[rows], k_send.at[n], k_recv.at[n], sibling)
         )
-    for n in range(SUBS):
-        rows = slab(core * HALF + n * SUB, SUB)
-        grad_ref[rows, :] = decoded(back[rows, :], GRADIENT)
+        update(core * HALF + n * SUB)
     for n in range(SUBS):
         back_core[n].wait_recv()
-        rows = slab((1 - core) * HALF + n * SUB, SUB)
-        grad_ref[rows, :] = decoded(back[rows, :], GRADIENT)
+        update((1 - core) * HALF + n * SUB)
     for copy in sent:
         copy.wait_send()
 
 
-def gradient(x, a, w, b, c, lin, sq, cube, y, r):
+def updated(samples, *arrays):
     dma = pltpu.SemaphoreType.DMA
     return pl.pallas_call(
-        kernel,
+        functools.partial(kernel, samples),
         out_shape=pltpu.VMEM((COLS, PH), F32),
-        in_specs=[pl.BlockSpec(memory_space=pltpu.HBM)] * 10,
+        in_specs=[pl.BlockSpec(memory_space=pltpu.HBM)] * len(arrays),
         out_specs=pl.BlockSpec(memory_space=pltpu.VMEM),
         scratch_shapes=[
             pltpu.VMEM((ROWS, COLS), BF16),
             pltpu.VMEM((ROWS, COLS), BF16),
             pltpu.VMEM((COLS, PH), F32),
+            pltpu.VMEM((COLS, PH), BF16),
             pltpu.VMEM((COLS, PH), BF16),
             pltpu.VMEM((SMALL, ROWS, PH), BF16),
             pltpu.VMEM((ROWS, COLS), BF16),
@@ -371,7 +388,7 @@
             pltpu.SemaphoreType.REGULAR((3,)),
             pltpu.SemaphoreType.REGULAR((3,)),
             pltpu.SemaphoreType.REGULAR((1,)),
-            dma((8,)),
+            dma((9,)),
             dma((CHUNKS, 2)),
             dma((CHUNKS,)), dma((CHUNKS,)),
             dma((2,)), dma((2,)),
@@ -391,14 +408,12 @@
         cost_estimate=pl.CostEstimate(
             flops=12 * ROWS * COLS * PH, bytes_accessed=5 * 2**20, transcendentals=0
         ),
-    )(x, a, w, b, c, lin, sq, cube, y, r)
-
-
-def shards(x, a, w, b, c, lin, sq, cube, y, r, grad_product):
-    grad = gradient(x, a, w, b, c, lin, sq, cube, y, r)
-    samples = x.shape[1] * lax.axis_size(SAMPLE)
-    whole = grad + grad_product[0].astype(F32)
-    return (w[0] - learn_rate / samples * whole)[None]
+    )(*arrays)
+
+
+def shards(*arrays):
+    samples = arrays[0].shape[1] * lax.axis_size(SAMPLE)
+    return updated(samples, *arrays)[None]
 
 
 def solution(mesh):

time: 61.2 us -> 60.8 us (level)
  other arithmetic: 1.14 us -> 0 us
  local copies, waits for them, and re-layouts: 0.01 us -> 0.97 us
    broadcast_in_dim x1 -> x0, other arithmetic: 1.14 us -> none  [shards(): return (w[0] - learn_rate / samples * whole)[None]]
    unnamed x4 -> x1, local copies, waits for them, and re-layouts: 0.01 us -> 0.97 us
where the time goes in v5:
time: 60.8 us; the launch traced here: 60.7 us
  Pallas kernels  59.7 us (98%)
  local copies, waits for them, and re-layouts  0.97 us (2%)
    pallas_call x1, Pallas kernels, updated(): pl.pallas_call(functools.partial(kernel, samples), out_shape=pltpu.VMEM((...  59.7 us

profile of v5, /device:TPU:1, one launch (start us, length us, event | category | flops | bytes accessed | tf_op | source)
XLA Modules:
  0.0 60.7 jit_solution(11169275792959766125)
XLA Ops:
  0.0 59.7 %shard_map.109 = f32[1024,256]{1,0:T(8,128)S(1)} custom-call(bf16[1,256,1024]{2,1,0:T(8,128)(2,1)} %x_ref.1, bf16[1,256,1024]{2,1,0:T(8,128)(2,1)} %a_ref.1, f32[1,1024,256]{2,1,0:T(8,128)} %w_ref.1, bf16[1,1024,256]{2,1,0:T(8,128)(2,1)} %b_ref.1, bf16[1,256,256]{2,1,0:T(8,128)(2,1)} %c_ref.1, bf16[1,256,256]{2,1,0:T(8,128)(2,1)} %lin_ref.1, ...), custom_call_target="tpu_custom_call" | custom-call | flops 805306368 | bytes 5242880 | tf_op jit(solution)/shard_map/pallas_call | solution.py:355
  59.7 1.0 %copy.13 = f32[1,1024,256]{2,1,0:T(8,128)} copy(f32[1,1024,256]{2,1,0:T(8,128)S(1)} %bitcast.1) | data formatting | bytes 2097152

commit v6 on v5

--- a/solution.py
+++ b/solution.py
@@ -154,6 +154,11 @@
         sent.append(copy)
         return copy
 
+    def settle(copies):
+        for copy in copies:
+            copy.wait_send()
+            sent[:] = [other for other in sent if other is not copy]
+
     def slab(first, size):
         return pl.ds(pl.multiple_of(first, size), size)
 
@@ -252,6 +257,7 @@
     shared_0 = share(0)
     turned(0)
     margins(2)
+    settle([weights, passed])
     margins(3)
     shared_1 = share(1)
     summed_0 = add_up(0, shared_0)
@@ -259,8 +265,11 @@
     opened_0 = residuals(0, summed_0)
     turned(1)
     gv[...] = jnp.dot(et[...], sv[SMALL - 1], preferred_element_type=F32)
+    settle(inputs + [packed] + shared_0)
     summed_1 = add_up(1, shared_1)
+    settle(shared_1 + [summed_0])
     opened_1 = residuals(1, summed_1)
+    settle(opened_0 + [summed_1])
     for copy in opened_0 + opened_1:
         copy.wait_recv()
     rr[ROWS:, :] = rr[:ROWS, :]
@@ -300,6 +309,7 @@
     ):
         step(n)
 
+    settle(opened_1 + crossing)
     lasts = []
     for n in range(SUBS):
         for copy in quarters[n]:
@@ -314,6 +324,7 @@
                 for d in (2, 1, 3)
             ]
         )
+    settle(sum(quarters, []))
     back_x = []
     for n in range(SUBS):
         for copy in lasts[n]:
@@ -334,6 +345,7 @@
         new_ref[rows, :] = wv[rows, :] - learn_rate / samples * whole
 
     load_p.wait()
+    settle(sum(lasts, []))
     back_core = []
     for n in range(SUBS):
         for copy in back_x[n]:
@@ -343,6 +355,7 @@
             remote(back.at[rows], back.at[rows], k_send.at[n], k_recv.at[n], sibling)
         )
         update(core * HALF + n * SUB)
+    settle(sum(back_x, []))
     for n in range(SUBS):
         back_core[n].wait_recv()
         update((1 - core) * HALF + n * SUB)

time: 60.8 us -> 60.7 us (level)
  no operation moved by 1% of the time
where the time goes in v6:
time: 60.7 us; the launch traced here: 60.6 us
  Pallas kernels  59.6 us (98%)
  local copies, waits for them, and re-layouts  0.97 us (2%)
    pallas_call x1, Pallas kernels, updated(): pl.pallas_call(functools.partial(kernel, samples), out_shape=pltpu.VMEM((...  59.6 us

profile of v6, /device:TPU:1, one launch (start us, length us, event | category | flops | bytes accessed | tf_op | source)
XLA Modules:
  0.0 60.6 jit_solution(14047987972483926083)
XLA Ops:
  0.0 59.6 %shard_map.109 = f32[1024,256]{1,0:T(8,128)S(1)} custom-call(bf16[1,256,1024]{2,1,0:T(8,128)(2,1)} %x_ref.1, bf16[1,256,1024]{2,1,0:T(8,128)(2,1)} %a_ref.1, f32[1,1024,256]{2,1,0:T(8,128)} %w_ref.1, bf16[1,1024,256]{2,1,0:T(8,128)(2,1)} %b_ref.1, bf16[1,256,256]{2,1,0:T(8,128)(2,1)} %c_ref.1, bf16[1,256,256]{2,1,0:T(8,128)(2,1)} %lin_ref.1, ...), custom_call_target="tpu_custom_call" | custom-call | flops 805306368 | bytes 5242880 | tf_op jit(solution)/shard_map/pallas_call | solution.py:368
  59.6 1.0 %copy.13 = f32[1,1024,256]{2,1,0:T(8,128)} copy(f32[1,1024,256]{2,1,0:T(8,128)S(1)} %bitcast.1) | data formatting | bytes 2097152

commit v7 on v5

--- a/solution.py
+++ b/solution.py
@@ -61,10 +61,10 @@
     samples,
     x_ref, a_ref, w_ref, b_ref, c_ref, lin_ref, sq_ref, cube_ref, y_ref, r_ref, p_ref,
     new_ref,
-    xv, av, wv, bv, pv, sv, mv, om, ev, et, ea, wm, ow, opened, zv, zc, zbuf, psum, pack, pbuf,
+    xv, av, wv, bv, pv, sv, mv, om, ev, et, ea, wm, ow, opened, zv, zc, zbuf, zfar, psum, pack, pbuf,
     rr, gv, gbuf, gc, xbuf, hbuf, back,
-    y_token, z_token, x_token, load_sem, first_sem, in_send, in_recv, wt_send, wt_recv, pk_send, pk_recv,
-    z_send, z_recv, p_send, p_recv, r_send, r_recv, g_send, g_recv, x_send, x_recv,
+    y_token, z_token, x_token, p_token, load_sem, first_sem, in_send, in_recv, wt_send, wt_recv, pk_send, pk_recv,
+    z_send, z_recv, q_send, q_recv, p_send, p_recv, r_send, r_recv, g_send, g_recv, x_send, x_recv,
     h_send, h_recv, e_send, e_recv, k_send, k_recv,
 ):
     party = lax.axis_index("party")
@@ -89,6 +89,9 @@
 
     def along_y(d):
         return at_place(f=lax.rem(feat + d, FEATS))
+
+    def across_y(d):
+        return at_place(p=1 - party, f=lax.rem(feat + d, FEATS))
 
     def along_x(d):
         return at_place(x=lax.rem(xi + d, 4))
@@ -185,6 +188,7 @@
     hear(1)
     pass_on(2)
     hear(2)
+    pl.semaphore_signal(p_token, inc=1, device_id=partner, device_id_type=MESH)
     weights.wait_recv()
     passed = remote(ow.at[my_half], ow.at[my_half], wt_send.at[1], wt_recv.at[1], sibling)
     passed.wait_recv()
@@ -216,15 +220,34 @@
         total = zv[slab(j * BLOCK + feat * PIECE, PIECE), :]
         for d in range(1, FEATS):
             total = total + decoded(zbuf[j, d], MARGIN)
-        psum[j, 0] = total
-        return remote(psum.at[j, 0], psum.at[j, 1], p_send.at[j], p_recv.at[j], partner)
-
-    def residuals(j, copy):
-        copy.wait_recv()
+        psum[0] = total
+        return remote(psum.at[0], psum.at[1], p_send.at[0], p_recv.at[0], partner)
+
+    def share_with_both():
+        own, far = {}, {}
+        for d in ALONG + (0,):
+            rows = slab(BLOCK + lax.rem(feat + d, FEATS) * PIECE, PIECE)
+            far[d] = remote(zc.at[rows], zfar.at[d], q_send.at[d], q_recv.at[d], across_y(d))
+            if d:
+                own[d] = remote(zc.at[rows], zbuf.at[1, d], z_send.at[1, d], z_recv.at[1, d], along_y(d))
+        return own, far
+
+    def both_sums(own, far):
+        own_sum = decoded(zc[slab(BLOCK + feat * PIECE, PIECE), :], MARGIN)
+        far[0].wait_recv()
+        far_sum = decoded(zfar[0], MARGIN)
+        for d in range(1, FEATS):
+            own[d].wait_recv()
+            own_sum = own_sum + decoded(zbuf[1, d], MARGIN)
+            far[d].wait_recv()
+            far_sum = far_sum + decoded(zfar[d], MARGIN)
+        return own_sum, far_sum
+
+    def residuals(j, own_sum, far_sum):
         own_rows = pl.ds(j * PIECE, PIECE)
         own = [pack[i, own_rows, :].astype(F32) for i in range(SMALL)]
         far = [pbuf[i, own_rows, :].astype(F32) for i in range(SMALL)]
-        own_margin, far_margin = psum[j, 0] + own[0], psum[j, 1] + far[0]
+        own_margin, far_margin = own_sum + own[0], far_sum + far[0]
         spread = (own_margin - own[1]) + (far_margin - far[1])
 
         def masked(s, margin, value):
@@ -252,15 +275,17 @@
     shared_0 = share(0)
     turned(0)
     margins(2)
+    pl.semaphore_wait(p_token, 1)
     margins(3)
-    shared_1 = share(1)
+    shared_1 = share_with_both()
     summed_0 = add_up(0, shared_0)
     packed.wait_recv()
-    opened_0 = residuals(0, summed_0)
+    summed_0.wait_recv()
+    opened_0 = residuals(0, psum[0], psum[1])
     turned(1)
     gv[...] = jnp.dot(et[...], sv[SMALL - 1], preferred_element_type=F32)
-    summed_1 = add_up(1, shared_1)
-    opened_1 = residuals(1, summed_1)
+    sums_1 = both_sums(*shared_1)
+    opened_1 = residuals(1, *sums_1)
     for copy in opened_0 + opened_1:
         copy.wait_recv()
     rr[ROWS:, :] = rr[:ROWS, :]
@@ -294,10 +319,14 @@
             ]
         )
 
-    for step, n in (
-        (cross, 0), (cross, 1), (keep, 0), (cross, 2), (keep, 1), (over_x, 0), (cross, 3),
-        (keep, 2), (over_x, 1), (keep, 3), (over_x, 2), (over_x, 3),
-    ):
+    steps = [(cross, 0), (cross, 1), (keep, 0)]
+    for n in range(SUBS):
+        if n + 2 < SUBS:
+            steps.append((cross, n + 2))
+        if n + 1 < SUBS:
+            steps.append((keep, n + 1))
+        steps.append((over_x, n))
+    for step, n in steps:
         step(n)
 
     lasts = []
@@ -375,7 +404,8 @@
             pltpu.VMEM((ROWS, PH), F32),
             pltpu.VMEM((ROWS, PH), BF16),
             pltpu.VMEM((BLOCKS, FEATS, PIECE, PH), BF16),
-            pltpu.VMEM((BLOCKS, 2, PIECE, PH), F32),
+            pltpu.VMEM((FEATS, PIECE, PH), BF16),
+            pltpu.VMEM((2, PIECE, PH), F32),
             pltpu.VMEM((SMALL, BLOCKS * PIECE, PH), BF16),
             pltpu.VMEM((SMALL, BLOCKS * PIECE, PH), BF16),
             pltpu.VMEM((2 * ROWS, PH), BF16),
@@ -388,13 +418,15 @@
             pltpu.SemaphoreType.REGULAR((3,)),
             pltpu.SemaphoreType.REGULAR((3,)),
             pltpu.SemaphoreType.REGULAR((1,)),
+            pltpu.SemaphoreType.REGULAR,
             dma((9,)),
             dma((CHUNKS, 2)),
             dma((CHUNKS,)), dma((CHUNKS,)),
             dma((2,)), dma((2,)),
             dma((1,)), dma((1,)),
             dma((BLOCKS, FEATS)), dma((BLOCKS, FEATS)),
-            dma((BLOCKS,)), dma((BLOCKS,)),
+            dma((FEATS,)), dma((FEATS,)),
+            dma((1,)), dma((1,)),
             dma((BLOCKS, FEATS)), dma((BLOCKS, FEATS)),
             dma((SUBS,)), dma((SUBS,)),
             dma((SUBS, 4)), dma((SUBS, 4)),

time: 60.8 us -> 60.3 us (level)
  no operation moved by 1% of the time
where the time goes in v7:
time: 60.3 us; the launch traced here: 60.2 us
  Pallas kernels  59.2 us (98%)
  local copies, waits for them, and re-layouts  0.97 us (2%)
    pallas_call x1, Pallas kernels, updated(): pl.pallas_call(functools.partial(kernel, samples), out_shape=pltpu.VMEM((...  59.2 us

profile of v7, /device:TPU:1, one launch (start us, length us, event | category | flops | bytes accessed | tf_op | source)
XLA Modules:
  0.0 60.2 jit_solution(12707070566280850449)
XLA Ops:
  0.0 59.2 %shard_map.109 = f32[1024,256]{1,0:T(8,128)S(1)} custom-call(bf16[1,256,1024]{2,1,0:T(8,128)(2,1)} %x_ref.1, bf16[1,256,1024]{2,1,0:T(8,128)(2,1)} %a_ref.1, f32[1,1024,256]{2,1,0:T(8,128)} %w_ref.1, bf16[1,1024,256]{2,1,0:T(8,128)(2,1)} %b_ref.1, bf16[1,256,256]{2,1,0:T(8,128)(2,1)} %c_ref.1, bf16[1,256,256]{2,1,0:T(8,128)(2,1)} %lin_ref.1, ...), custom_call_target="tpu_custom_call" | custom-call | flops 805306368 | bytes 5242880 | tf_op jit(solution)/shard_map/pallas_call | solution.py:384
  59.2 1.0 %copy.13 = f32[1,1024,256]{2,1,0:T(8,128)} copy(f32[1,1024,256]{2,1,0:T(8,128)S(1)} %bitcast.1) | data formatting | bytes 2097152

commit v8 on v7

--- a/solution.py
+++ b/solution.py
@@ -290,19 +290,24 @@
         copy.wait_recv()
     rr[ROWS:, :] = rr[:ROWS, :]
 
-    def terms(first):
-        rows = slab(first, SUB)
-        return gv[rows, :] + jnp.dot(ea[rows, :], rr[...], preferred_element_type=F32)
+    def terms(first, size):
+        rows = pl.ds(pl.multiple_of(first, SUB), size)
+        gv[rows, :] += jnp.dot(ea[rows, :], rr[...], preferred_element_type=F32)
 
     crossing, quarters = [], []
+    their, own = (1 - core) * HALF, core * HALF
 
     def cross(n):
-        rows = slab((1 - core) * HALF + n * SUB, SUB)
-        gv[rows, :] = terms((1 - core) * HALF + n * SUB)
+        rows = slab(their + n * SUB, SUB)
         crossing.append(remote(gv.at[rows], gbuf.at[n], g_send.at[n], g_recv.at[n], sibling))
 
-    def keep(n):
-        gv[slab(core * HALF + n * SUB, SUB), :] = terms(core * HALF + n * SUB)
+    terms(their, SUB)
+    cross(0)
+    terms(their + SUB, HALF - SUB)
+    for n in range(1, SUBS):
+        cross(n)
+    terms(own, SUB)
+    terms(own + SUB, HALF - SUB)
 
     def over_x(n):
         crossing[n].wait_recv()
@@ -319,15 +324,8 @@
             ]
         )
 
-    steps = [(cross, 0), (cross, 1), (keep, 0)]
     for n in range(SUBS):
-        if n + 2 < SUBS:
-            steps.append((cross, n + 2))
-        if n + 1 < SUBS:
-            steps.append((keep, n + 1))
-        steps.append((over_x, n))
-    for step, n in steps:
-        step(n)
+        over_x(n)
 
     lasts = []
     for n in range(SUBS):
@@ -372,9 +370,11 @@
             remote(back.at[rows], back.at[rows], k_send.at[n], k_recv.at[n], sibling)
         )
         update(core * HALF + n * SUB)
-    for n in range(SUBS):
-        back_core[n].wait_recv()
-        update((1 - core) * HALF + n * SUB)
+        if n > 0:
+            back_core[n - 1].wait_recv()
+            update((1 - core) * HALF + (n - 1) * SUB)
+    back_core[SUBS - 1].wait_recv()
+    update((1 - core) * HALF + (SUBS - 1) * SUB)
     for copy in sent:
         copy.wait_send()
 

time: 60.3 us -> 60.3 us (level)
  no operation moved by 1% of the time
where the time goes in v8:
time: 60.3 us; the launch traced here: 60.2 us
  Pallas kernels  59.2 us (98%)
  local copies, waits for them, and re-layouts  0.97 us (2%)
    pallas_call x1, Pallas kernels, updated(): pl.pallas_call(functools.partial(kernel, samples), out_shape=pltpu.VMEM((...  59.2 us

profile of v8, /device:TPU:1, one launch (start us, length us, event | category | flops | bytes accessed | tf_op | source)
XLA Modules:
  0.0 60.2 jit_solution(17488191920691735909)
XLA Ops:
  0.0 59.2 %shard_map.109 = f32[1024,256]{1,0:T(8,128)S(1)} custom-call(bf16[1,256,1024]{2,1,0:T(8,128)(2,1)} %x_ref.1, bf16[1,256,1024]{2,1,0:T(8,128)(2,1)} %a_ref.1, f32[1,1024,256]{2,1,0:T(8,128)} %w_ref.1, bf16[1,1024,256]{2,1,0:T(8,128)(2,1)} %b_ref.1, bf16[1,256,256]{2,1,0:T(8,128)(2,1)} %c_ref.1, bf16[1,256,256]{2,1,0:T(8,128)(2,1)} %lin_ref.1, ...), custom_call_target="tpu_custom_call" | custom-call | flops 805306368 | bytes 5242880 | tf_op jit(solution)/shard_map/pallas_call | solution.py:384
  59.2 1.0 %copy.13 = f32[1,1024,256]{2,1,0:T(8,128)} copy(f32[1,1024,256]{2,1,0:T(8,128)S(1)} %bitcast.1) | data formatting | bytes 2097152

commit v9 on v8

--- a/solution.py
+++ b/solution.py
@@ -327,8 +327,10 @@
     for n in range(SUBS):
         over_x(n)
 
-    lasts = []
-    for n in range(SUBS):
+    lasts, passing, back_x = [], [], []
+    below, above = lax.rem(hi + 3, 4), lax.rem(hi + 1, 4)
+
+    def over_z(n):
         for copy in quarters[n]:
             copy.wait_recv()
         total = gbuf[n, slab(xi * QUARTER, QUARTER), :]
@@ -338,12 +340,21 @@
         lasts.append(
             [
                 remote(hbuf.at[n, hi], hbuf.at[n, hi], h_send.at[n, d], h_recv.at[n, d], along_z(d))
-                for d in (2, 1, 3)
+                for d in (1, 3)
             ]
         )
-    back_x = []
-    for n in range(SUBS):
-        for copy in lasts[n]:
+
+    def pass_along(n):
+        lasts[n][0].wait_recv()
+        first = hbuf.at[n, below, pl.ds(0, QUARTER // 2)]
+        upward = remote(first, first, h_send.at[n, 0], h_recv.at[n, 0], along_z(1))
+        lasts[n][1].wait_recv()
+        second = hbuf.at[n, above, pl.ds(QUARTER // 2, QUARTER // 2)]
+        downward = remote(second, second, h_send.at[n, 2], h_recv.at[n, 2], along_z(3))
+        passing.append([upward, downward])
+
+    def return_over_x(n):
+        for copy in passing[n]:
             copy.wait_recv()
         total = decoded(hbuf[n, 0], GRADIENT) + decoded(hbuf[n, 1], GRADIENT)
         total = total + (decoded(hbuf[n, 2], GRADIENT) + decoded(hbuf[n, 3], GRADIENT))
@@ -355,6 +366,14 @@
                 for d in (2, 1, 3)
             ]
         )
+
+    for n in range(SUBS + 4):
+        if n < SUBS:
+            over_z(n)
+        if 2 <= n < SUBS + 2:
+            pass_along(n - 2)
+        if n >= 4:
+            return_over_x(n - 4)
     def update(first):
         rows = slab(first, SUB)
         whole = decoded(back[rows, :], GRADIENT) + pv[rows, :].astype(F32)

time: 60.3 us -> 63.3 us (1.050)
  Pallas kernels: 59.2 us -> 62.2 us
    pallas_call x1, Pallas kernels: 59.2 us -> 62.2 us  [updated(): pl.pallas_call(functools.partial(kernel, samples), out_shape=pltpu.VMEM((...]
where the time goes in v9:
time: 63.3 us; the launch traced here: 63.1 us
  Pallas kernels  62.2 us (98%)
  local copies, waits for them, and re-layouts  0.97 us (2%)
    pallas_call x1, Pallas kernels, updated(): pl.pallas_call(functools.partial(kernel, samples), out_shape=pltpu.VMEM((...  62.2 us

profile of v9, /device:TPU:1, one launch (start us, length us, event | category | flops | bytes accessed | tf_op | source)
XLA Modules:
  0.0 63.1 jit_solution(16465394613836445516)
XLA Ops:
  0.0 62.2 %shard_map.109 = f32[1024,256]{1,0:T(8,128)S(1)} custom-call(bf16[1,256,1024]{2,1,0:T(8,128)(2,1)} %x_ref.1, bf16[1,256,1024]{2,1,0:T(8,128)(2,1)} %a_ref.1, f32[1,1024,256]{2,1,0:T(8,128)} %w_ref.1, bf16[1,1024,256]{2,1,0:T(8,128)(2,1)} %b_ref.1, bf16[1,256,256]{2,1,0:T(8,128)(2,1)} %c_ref.1, bf16[1,256,256]{2,1,0:T(8,128)(2,1)} %lin_ref.1, ...), custom_call_target="tpu_custom_call" | custom-call | flops 805306368 | bytes 5242880 | tf_op jit(solution)/shard_map/pallas_call | solution.py:403
  62.2 1.0 %copy.13 = f32[1,1024,256]{2,1,0:T(8,128)} copy(f32[1,1024,256]{2,1,0:T(8,128)S(1)} %bitcast.1) | data formatting | bytes 2097152

commit v10 on v8

--- a/solution.py
+++ b/solution.py
@@ -96,6 +96,9 @@
     def along_x(d):
         return at_place(x=lax.rem(xi + d, 4))
 
+    def across_x(d):
+        return at_place(x=lax.rem(xi + d, 4), c=1 - core)
+
     def along_z(d):
         return at_place(h=lax.rem(hi + d, 4))
 
@@ -341,7 +344,7 @@
                 for d in (2, 1, 3)
             ]
         )
-    back_x = []
+    back_x, back_core = [], []
     for n in range(SUBS):
         for copy in lasts[n]:
             copy.wait_recv()
@@ -355,26 +358,25 @@
                 for d in (2, 1, 3)
             ]
         )
+        back_core.append(
+            [
+                remote(back.at[rows], back.at[rows], k_send.at[n, d], k_recv.at[n, d], across_x(d))
+                for d in (2, 1, 3, 0)
+            ]
+        )
     def update(first):
         rows = slab(first, SUB)
         whole = decoded(back[rows, :], GRADIENT) + pv[rows, :].astype(F32)
         new_ref[rows, :] = wv[rows, :] - learn_rate / samples * whole
 
     load_p.wait()
-    back_core = []
     for n in range(SUBS):
         for copy in back_x[n]:
             copy.wait_recv()
-        rows = slab(core * HALF + n * SUB, SUB)
-        back_core.append(
-            remote(back.at[rows], back.at[rows], k_send.at[n], k_recv.at[n], sibling)
-        )
         update(core * HALF + n * SUB)
-        if n > 0:
-            back_core[n - 1].wait_recv()
-            update((1 - core) * HALF + (n - 1) * SUB)
-    back_core[SUBS - 1].wait_recv()
-    update((1 - core) * HALF + (SUBS - 1) * SUB)
+        for copy in back_core[n]:
+            copy.wait_recv()
+        update((1 - core) * HALF + n * SUB)
     for copy in sent:
         copy.wait_send()
 
@@ -432,7 +434,7 @@
             dma((SUBS, 4)), dma((SUBS, 4)),
             dma((SUBS, 4)), dma((SUBS, 4)),
             dma((SUBS, 4)), dma((SUBS, 4)),
-            dma((SUBS,)), dma((SUBS,)),
+            dma((SUBS, 4)), dma((SUBS, 4)),
         ],
         compiler_params=pltpu.CompilerParams(
             collective_id=0, has_side_effects=True, vmem_limit_bytes=60 * 2**20

time: 60.3 us -> 59.8 us (level)
  no operation moved by 1% of the time
where the time goes in v10:
time: 59.8 us; the launch traced here: 59.6 us
  Pallas kernels  58.7 us (98%)
  local copies, waits for them, and re-layouts  0.97 us (2%)
    pallas_call x1, Pallas kernels, updated(): pl.pallas_call(functools.partial(kernel, samples), out_shape=pltpu.VMEM((...  58.7 us

profile of v10, /device:TPU:1, one launch (start us, length us, event | category | flops | bytes accessed | tf_op | source)
XLA Modules:
  0.0 59.6 jit_solution(8647566144698301735)
XLA Ops:
  0.0 58.7 %shard_map.109 = f32[1024,256]{1,0:T(8,128)S(1)} custom-call(bf16[1,256,1024]{2,1,0:T(8,128)(2,1)} %x_ref.1, bf16[1,256,1024]{2,1,0:T(8,128)(2,1)} %a_ref.1, f32[1,1024,256]{2,1,0:T(8,128)} %w_ref.1, bf16[1,1024,256]{2,1,0:T(8,128)(2,1)} %b_ref.1, bf16[1,256,256]{2,1,0:T(8,128)(2,1)} %c_ref.1, bf16[1,256,256]{2,1,0:T(8,128)(2,1)} %lin_ref.1, ...), custom_call_target="tpu_custom_call" | custom-call | flops 805306368 | bytes 5242880 | tf_op jit(solution)/shard_map/pallas_call | solution.py:386
  58.7 1.0 %copy.13 = f32[1,1024,256]{2,1,0:T(8,128)} copy(f32[1,1024,256]{2,1,0:T(8,128)S(1)} %bitcast.1) | data formatting | bytes 2097152

commit v11 on v10

--- a/solution.py
+++ b/solution.py
@@ -183,7 +183,6 @@
     for i in range(SMALL):
         for j in range(BLOCKS):
             pack[i, pl.ds(j * PIECE, PIECE), :] = sv[i, slab(j * BLOCK + feat * PIECE, PIECE), :]
-    packed = remote(pack, pbuf, pk_send.at[0], pk_recv.at[0], partner)
 
     ea[:, ROWS:] = av[...].T
     hear(0)
@@ -281,6 +280,7 @@
     pl.semaphore_wait(p_token, 1)
     margins(3)
     shared_1 = share_with_both()
+    packed = remote(pack, pbuf, pk_send.at[0], pk_recv.at[0], partner)
     summed_0 = add_up(0, shared_0)
     packed.wait_recv()
     summed_0.wait_recv()

time: 59.8 us -> 58.7 us (0.982)
  Pallas kernels: 58.7 us -> 57.7 us
    pallas_call x1, Pallas kernels: 58.7 us -> 57.7 us  [updated(): pl.pallas_call(functools.partial(kernel, samples), out_shape=pltpu.VMEM((...]
where the time goes in v11:
time: 58.7 us; the launch traced here: 58.6 us
  Pallas kernels  57.7 us (98%)
  local copies, waits for them, and re-layouts  0.97 us (2%)
    pallas_call x1, Pallas kernels, updated(): pl.pallas_call(functools.partial(kernel, samples), out_shape=pltpu.VMEM((...  57.7 us

profile of v11, /device:TPU:1, one launch (start us, length us, event | category | flops | bytes accessed | tf_op | source)
XLA Modules:
  0.0 58.6 jit_solution(5782181838076168040)
XLA Ops:
  0.0 57.7 %shard_map.109 = f32[1024,256]{1,0:T(8,128)S(1)} custom-call(bf16[1,256,1024]{2,1,0:T(8,128)(2,1)} %x_ref.1, bf16[1,256,1024]{2,1,0:T(8,128)(2,1)} %a_ref.1, f32[1,1024,256]{2,1,0:T(8,128)} %w_ref.1, bf16[1,1024,256]{2,1,0:T(8,128)(2,1)} %b_ref.1, bf16[1,256,256]{2,1,0:T(8,128)(2,1)} %c_ref.1, bf16[1,256,256]{2,1,0:T(8,128)(2,1)} %lin_ref.1, ...), custom_call_target="tpu_custom_call" | custom-call | flops 805306368 | bytes 5242880 | tf_op jit(solution)/shard_map/pallas_call | solution.py:386
  57.7 1.0 %copy.13 = f32[1,1024,256]{2,1,0:T(8,128)} copy(f32[1,1024,256]{2,1,0:T(8,128)S(1)} %bitcast.1) | data formatting | bytes 2097152

commit v12 on v11

--- a/solution.py
+++ b/solution.py
@@ -282,11 +282,11 @@
     shared_1 = share_with_both()
     packed = remote(pack, pbuf, pk_send.at[0], pk_recv.at[0], partner)
     summed_0 = add_up(0, shared_0)
+    turned(1)
+    gv[...] = jnp.dot(et[...], sv[SMALL - 1], preferred_element_type=F32)
     packed.wait_recv()
     summed_0.wait_recv()
     opened_0 = residuals(0, psum[0], psum[1])
-    turned(1)
-    gv[...] = jnp.dot(et[...], sv[SMALL - 1], preferred_element_type=F32)
     sums_1 = both_sums(*shared_1)
     opened_1 = residuals(1, *sums_1)
     for copy in opened_0 + opened_1:

time: 58.7 us -> 58.5 us (level)
  no operation moved by 1% of the time
where the time goes in v12:
time: 58.5 us; the launch traced here: 58.4 us
  Pallas kernels  57.4 us (98%)
  local copies, waits for them, and re-layouts  0.97 us (2%)
    pallas_call x1, Pallas kernels, updated(): pl.pallas_call(functools.partial(kernel, samples), out_shape=pltpu.VMEM((...  57.4 us

profile of v12, /device:TPU:1, one launch (start us, length us, event | category | flops | bytes accessed | tf_op | source)
XLA Modules:
  0.0 58.4 jit_solution(16911110667780668682)
XLA Ops:
  0.0 57.4 %shard_map.109 = f32[1024,256]{1,0:T(8,128)S(1)} custom-call(bf16[1,256,1024]{2,1,0:T(8,128)(2,1)} %x_ref.1, bf16[1,256,1024]{2,1,0:T(8,128)(2,1)} %a_ref.1, f32[1,1024,256]{2,1,0:T(8,128)} %w_ref.1, bf16[1,1024,256]{2,1,0:T(8,128)(2,1)} %b_ref.1, bf16[1,256,256]{2,1,0:T(8,128)(2,1)} %c_ref.1, bf16[1,256,256]{2,1,0:T(8,128)(2,1)} %lin_ref.1, ...), custom_call_target="tpu_custom_call" | custom-call | flops 805306368 | bytes 5242880 | tf_op jit(solution)/shard_map/pallas_call | solution.py:386
  57.4 1.0 %copy.13 = f32[1,1024,256]{2,1,0:T(8,128)} copy(f32[1,1024,256]{2,1,0:T(8,128)S(1)} %bitcast.1) | data formatting | bytes 2097152
